TPU v7x, 256 devices: a whole 4x4x8 slice. The times are simulated.
256 devices in a mesh: panel: 32 (over x, z), obs: 8 (over y, core).
Axes of the slice: x: 4, y: 4, z: 8, core: 2. Of those that a mesh axis runs over, the one named last changes fastest.
Arguments:
- series: float32 [256, 5, 65536], P('obs', None, 'panel'), may hold values from -6 to 6
- panel_pos: float32 [3, 65536], P(None, 'panel'), may hold values from -1 to 1
- panel_area: float32 [3, 65536], P(None, 'panel'), may hold values from -3 to 3
- observers: float32 [3, 1024], replicated, may hold values from -4 to 4, as said below
- owner: int32 [65536], P('panel'), may hold values from -1 to 31, as said below
Outputs:
- spectrum: float32 [1024, 2, 32], P('panel', None, 'obs')
Inputs may be any that keep to these rules, and one draw needn't show every extreme that they name: `owner`: on each device the live slots come first and the empty ones hold -1; the number of live slots of a device is a multiple of 32, and its live slots name every device of the panel axis equally often, at most 64 times, a device with all 2048 slots live reaching that. In all, every device is named by exactly 1024 slots. `observers`: the first coordinate of every observer lies between 2 and 4, the other two between -4 and 4.
All inputs are finite; a program needn't handle non-finite values.
Results may differ from a plain program's by a relative error of at most 0.0003.
Values sent between devices are 32-bit elements; how exact they have to be, the bound alone decides.
No kernel may reach another device: no remote copies, remote signals or barrier semaphores. Data moves between devices by JAX's collectives and lax.ppermute only.
A program may use at most 64 MiB of HBM per device.

v0:
```python
import math

import jax
import jax.numpy as jnp
from jax import lax
from jax.sharding import PartitionSpec as P

TIME = 256
FREQ = 32
PAN_DEV = 1024


PRECISE = lax.Precision.HIGHEST
MACH_NUMBER = 0.3
DENSITY = 1.0
SAMPLE_SPACING = 0.04
FOUR_PI = 4.0 * math.pi


def fourier_rows(harmonic, instant):
    turns = harmonic[:, None] * instant[None, :] % TIME
    angle = turns.astype(jnp.float32) * (2.0 * math.pi / TIME)
    return jnp.stack([jnp.cos(angle) * (2.0 / TIME), -jnp.sin(angle) * (2.0 / TIME)], axis=1)


def panel_columns(band, position, area_vec, wavenumber):
    real_part = band[0:5]
    imag_part = band[5:10]
    convect = MACH_NUMBER * area_vec[0]
    flux_real = (
        DENSITY
        * (area_vec[0] * real_part[1] + area_vec[1] * real_part[2] + area_vec[2] * real_part[3])
        + convect * real_part[0]
    )
    flux_imag = (
        DENSITY
        * (area_vec[0] * imag_part[1] + area_vec[1] * imag_part[2] + area_vec[2] * imag_part[3])
        + convect * imag_part[0]
    )
    mono_real = -wavenumber * flux_imag
    mono_imag = wavenumber * flux_real
    load_real = [
        area_vec[axis_id] * real_part[4] + DENSITY * convect * real_part[1 + axis_id]
        for axis_id in range(3)
    ]
    load_imag = [
        area_vec[axis_id] * imag_part[4] + DENSITY * convect * imag_part[1 + axis_id]
        for axis_id in range(3)
    ]
    moment_real = -(
        position[0] * load_real[0] + position[1] * load_real[1] + position[2] * load_real[2]
    )
    moment_imag = -(
        position[0] * load_imag[0] + position[1] * load_imag[1] + position[2] * load_imag[2]
    )
    cols_real = jnp.stack([mono_real] + load_real + [moment_real], axis=1)
    cols_imag = jnp.stack([mono_imag] + load_imag + [moment_imag], axis=1)
    return (cols_real, cols_imag)


def propagate(listener, position, cols_real, cols_imag, wavenumber):
    delta_x = listener[0][:, None] - position[0][None, :]
    delta_y = listener[1][:, None] - position[1][None, :]
    delta_z = listener[2][:, None] - position[2][None, :]
    distance = jnp.sqrt(delta_x * delta_x + delta_y * delta_y + delta_z * delta_z)
    phase_angle = wavenumber * distance
    inverse = 1.0 / (FOUR_PI * distance)
    green_real = jnp.cos(phase_angle) * inverse
    green_imag = -jnp.sin(phase_angle) * inverse
    inverse_square = 1.0 / (distance * distance)
    dipole_real = (green_real - phase_angle * green_imag) * inverse_square
    dipole_imag = (green_imag + phase_angle * green_real) * inverse_square
    lever_real = (
        listener[0][:, None] * cols_real[:, 1][None, :]
        + listener[1][:, None] * cols_real[:, 2][None, :]
        + listener[2][:, None] * cols_real[:, 3][None, :]
        + cols_real[:, 4][None, :]
    )
    lever_imag = (
        listener[0][:, None] * cols_imag[:, 1][None, :]
        + listener[1][:, None] * cols_imag[:, 2][None, :]
        + listener[2][:, None] * cols_imag[:, 3][None, :]
        + cols_imag[:, 4][None, :]
    )
    mono_real = cols_real[:, 0][None, :]
    mono_imag = cols_imag[:, 0][None, :]
    term_real = (
        green_real * mono_real
        - green_imag * mono_imag
        + dipole_real * lever_real
        - dipole_imag * lever_imag
    )
    term_imag = (
        green_real * mono_imag
        + green_imag * mono_real
        + dipole_real * lever_imag
        + dipole_imag * lever_real
    )
    return jnp.stack([jnp.sum(term_real, axis=1), jnp.sum(term_imag, axis=1)], axis=1)


def frequency_terms(series_local):
    step_count = series_local.shape[0]
    field_count = series_local.shape[1]
    column_count = series_local.shape[2]
    instant = lax.axis_index("obs") * step_count + jnp.arange(step_count, dtype=jnp.int32)
    harmonic = (
        jnp.int32(0)
        + 1
        + jnp.arange(FREQ // lax.axis_size("obs") * lax.axis_size("obs"), dtype=jnp.int32)
    )
    rows_now = fourier_rows(harmonic, instant)
    product = jnp.einsum("kct,tfs->kcfs", rows_now, series_local, precision=PRECISE)
    return lax.psum_scatter(
        product.reshape(
            FREQ // lax.axis_size("obs") * lax.axis_size("obs"), 2 * field_count, column_count
        ),
        "obs",
        scatter_dimension=0,
        tiled=True,
    )


def pack_index(owner, groups, capacity):
    slot_count = owner.shape[0]
    onehot = (owner[:, None] == jnp.arange(groups, dtype=jnp.int32)[None, :]).astype(jnp.int32)
    ranking = jnp.sum(onehot * (jnp.cumsum(onehot, axis=0) - 1), axis=1)
    target = jnp.where(owner >= 0, owner * capacity + ranking, groups * capacity)
    source_of = jnp.full((groups * capacity,), slot_count, jnp.int32)
    return source_of.at[target].set(jnp.arange(slot_count, dtype=jnp.int32), mode="drop")


def pack_rows(values, source_of, groups, capacity):
    packed = jnp.take(values, source_of, axis=1, mode="fill", fill_value=0)
    return packed.reshape(values.shape[0], groups, capacity)


def unpack_index(flags, groups, capacity):
    arrived = jnp.sum(flags, axis=1).astype(jnp.int32)
    finish = jnp.cumsum(arrived)
    starts = finish - arrived
    row_ids = jnp.arange(PAN_DEV, dtype=jnp.int32)
    source = jnp.sum((finish[None, :] <= row_ids[:, None]).astype(jnp.int32), axis=1)
    chosen = (source[:, None] == jnp.arange(groups, dtype=jnp.int32)[None, :]).astype(jnp.int32)
    start_row = jnp.sum(chosen * starts[None, :], axis=1)
    return source * capacity + row_ids - start_row


def take_rows(received, picked):
    flat = received.reshape(received.shape[0], received.shape[1] * received.shape[2])
    return jnp.take(flat, picked, axis=1)


def on_device(series, panel_pos, panel_area, observers, owner):
    groups = lax.axis_size("panel")
    slot_count = owner.shape[0]
    capacity = slot_count // groups
    field_count = series.shape[1]
    step_count = series.shape[0]
    live_flag = (owner >= 0).astype(jnp.float32)
    geometry = jnp.concatenate(
        [panel_pos, panel_area * live_flag[None, :], live_flag[None, :]], axis=0
    )
    source_of = pack_index(owner, groups, capacity)
    flat_series = series.reshape(step_count * field_count, slot_count)
    moved, geometry_in = (
        lax.all_to_all(
            pack_rows(flat_series, source_of, groups, capacity),
            "panel",
            split_axis=1,
            concat_axis=1,
            tiled=True,
        ),
        lax.all_to_all(
            pack_rows(geometry, source_of, groups, capacity),
            "panel",
            split_axis=1,
            concat_axis=1,
            tiled=True,
        ),
    )
    picked = unpack_index(geometry_in[6], groups, capacity)
    spectra = frequency_terms(take_rows(moved, picked).reshape(step_count, field_count, PAN_DEV))
    placed = take_rows(geometry_in, picked)
    position = placed[0:3]
    area_vec = placed[3:6]
    band_count = spectra.shape[0]
    first_band = lax.axis_index("obs") * band_count
    prepared = []
    for band_index in range(band_count):
        wavenumber = (first_band + band_index + 1).astype(jnp.float32) * (
            2.0 * math.pi / (TIME * SAMPLE_SPACING)
        )
        cols_real, cols_imag = panel_columns(spectra[band_index], position, area_vec, wavenumber)
        prepared.append((wavenumber, cols_real, cols_imag))
    results = [propagate(observers, position, entry[1], entry[2], entry[0]) for entry in prepared]
    return lax.psum_scatter(jnp.stack(results, axis=2), "panel", scatter_dimension=0, tiled=True)


def solution(mesh):
    in_specs = (P("obs", None, "panel"), P(None, "panel"), P(None, "panel"), P(), P("panel"))
    out_specs = P("panel", None, "obs")
    return jax.shard_map(
        on_device, mesh=mesh, in_specs=in_specs, out_specs=out_specs, check_vma=False
    )
```

profile of v0, /device:TPU:8, one launch (start us, length us, event | category | flops | bytes accessed | tf_op | source)
XLA Modules:
  0.0 485.0 jit_solution(7023657240051383643)
XLA Ops:
  6.5 0.8 fusion.32
  7.3 0.7 fusion.9
  8.0 9.1 %reduce-window.14 = s32[32,16,128]{2,1,0:T(8,128)S(1)} reduce-window(s32[32,16,128]{2,1,0:T(8,128)S(1)} %fusion.9, s32[]{:T(128)} %constant.71.clone.1), window={size=1x1x128 pad=0_0x0_0x127_0}, to_apply=%region_0.0 | reduce-window | flops 8323072 | bytes 524292 | tf_op jit(solution)/shard_map/reduce-window
  17.1 0.1 slice.487
  17.2 0.2 copy.303
  17.5 0.2 reduce-window.18
  17.7 0.1 add_add_fusion.8
  17.8 0.1 fusion.8
  18.0 8.0 %scatter_custom_fusion = s32[2048]{0:T(1024)S(1)} fusion(s32[2048]{0:T(1024)S(1)} %compare_select_fusion.2, s32[2048]{0:T(1024)S(1)} %iota.32, s32[]{:T(128)} %constant.70.clone.1), kind=kCustom, calls=%fused_computation.179 | custom fusion | bytes 8196 | tf_op jit(solution)/shard_map/scatter | solution.py:130
  26.1 0.4 copy.291
  26.5 5.5 %gather_fusion = f32[2048,7]{1,0:T(8,128)S(1)} fusion(f32[7,2048]{0,1:T(8,128)S(1)} %copy.291, s32[2048]{0:T(1024)S(1)} %fusion.15), kind=kCustom, calls=%fused_computation | custom fusion | bytes 122880 | tf_op jit(solution)/shard_map/jit(_take)/gather | solution.py:134
  32.0 0.4 copy.292
  32.4 0.1 broadcast_in_dim.63
  32.5 0.8 reshape.521
  33.2 11.3 %all-to-all-start = ((f32[32,1,448]{2,1,0:T(1,128)}), f32[32,1,448]{2,1,0:T(1,128)S(1)}, u32[]{:S(2)}, u32[]{:S(2)}) async-start(f32[32,1,448]{2,1,0:T(1,128)} %reshape.521), calls=%async_computation | async-start | bytes 131072 | tf_op jit(solution)/shard_map/all_to_all | solution.py:174
  44.6 0.8 copy.296
  45.4 0.2 reshape.468
  45.6 0.8 copy.297
  46.5 8.6 %gather_fusion.2 = f32[2048,160]{1,0:T(8,128)} fusion(f32[160,2048]{0,1:T(8,128)S(1)} %copy.297, s32[2048]{0:T(1024)S(1)} %fusion.15), kind=kCustom, calls=%fused_computation.2 | custom fusion | bytes 2629632 | tf_op jit(solution)/shard_map/jit(_take)/gather | solution.py:134
  55.0 3.3 broadcast_select_fusion
  58.3 9.8 %all-to-all-start.1 = ((f32[160,32,64]{0,2,1:T(8,128)}), f32[160,32,64]{0,2,1:T(8,128)S(1)}, u32[]{:S(2)}, u32[]{:S(2)}) async-start(f32[160,32,64]{0,2,1:T(8,128)} %broadcast_select_fusion), calls=%async_computation.1 | async-start | bytes 4194304 | tf_op jit(solution)/shard_map/all_to_all | solution.py:167
  68.1 0.0 reduce-scatter.5.cloned.1.call-start
  68.2 0.2 cosine_multiply_fusion.4
  68.3 0.5 broadcast.549
  68.8 0.8 reduce.2
  69.6 0.1 reshape.522
  69.7 0.3 slice_reduce_fusion
  70.1 0.1 copy.293
  70.2 0.1 reduce-window.19
  70.2 0.1 reduce.1
  70.3 0.1 convert_reduce_fusion
  70.4 0.1 select_reduce_fusion
  70.6 47.2 %all-to-all-done.1 = f32[160,32,64]{0,2,1:T(8,128)S(1)} async-done(((f32[160,32,64]{0,2,1:T(8,128)}), f32[160,32,64]{0,2,1:T(8,128)S(1)}, u32[]{:S(2)}, u32[]{:S(2)}) %all-to-all-start.1) | async-done | bytes 1310752 | tf_op jit(solution)/shard_map/all_to_all | solution.py:167
  117.8 3.5 gather_fusion.3
  121.2 0.3 copy.298
  121.5 0.1 gather.28
  121.6 0.2 broadcast_select_fusion.1
  121.8 1.5 fusion.4
  123.3 2.1 copy.300
  125.5 0.0 reduce-scatter.5.cloned.1.call-update
  125.5 0.3 reduce-scatter.7.cloned.1.call-start
  125.9 0.4 copy.294
  126.3 2.8 gather_fusion.1
  129.1 0.2 copy.295
  129.3 26.8 %reduce-scatter.5.cloned.1.call-done = f32[4,10,1024]{2,1,0:T(8,128)} async-done(((f32[32,10,1024]{2,1,0:T(8,128)}), f32[4,10,1024]{2,1,0:T(8,128)}) %reduce-scatter.5.cloned.1.call-update) | async-done | bytes 163856 | tf_op jit(solution)/shard_map/reduce_scatter | solution.py:114
  156.1 0.9 add_negate_fusion
  157.0 0.9 add_negate_fusion.1
  157.9 1.0 add_negate_fusion.4
  158.9 1.0 add_negate_fusion.6
  159.9 1.0 fusion.35
  160.9 23.2 %subtract_reduce_fusion = (f32[1024]{0:T(1024)S(1)}, f32[1024]{0:T(1024)S(1)}) fusion(f32[1024]{0:T(1024)S(1)} %bitcast.449, f32[1024]{0:T(1024)S(1)} %bitcast.452, f32[1024]{0:T(1024)S(1)} %bitcast.451, f32[1024]{0:T(1024)S(1)} %bitcast.450, f32[1024]{0:T(1024)S(1)} %bitcast.453, f32[1024]{0:T(1024)S(1)} %bitcast.456, f32[1024]{0:T(1024)S(1)} %bitcast.455, ...), kind=kLoop, calls=%fused_computation.6 | loop fusion | flops 52426752 | bytes 73732 | tf_op jit(solution)/shard_map/reduce_sum | solution.py:99
  184.1 1.0 add_negate_fusion.3
  185.1 0.9 add_negate_fusion.2
  186.0 23.7 %subtract_reduce_fusion.1 = (f32[1024]{0:T(1024)S(1)}, f32[1024]{0:T(1024)S(1)}) fusion(f32[1024]{0:T(1024)S(1)} %bitcast.496, f32[1024]{0:T(1024)S(1)} %bitcast.499, f32[1024]{0:T(1024)S(1)} %bitcast.498, f32[1024]{0:T(1024)S(1)} %bitcast.497, f32[1024]{0:T(1024)S(1)} %bitcast.492, f32[1024]{0:T(1024)S(1)} %bitcast.495, f32[1024]{0:T(1024)S(1)} %bitcast.494, ...), kind=kLoop, calls=%fused_computation.14 | loop fusion | flops 52426752 | bytes 73732 | tf_op jit(solution)/shard_map/reduce_sum | solution.py:99
  209.8 1.0 add_negate_fusion.5
  210.8 1.0 add_negate_fusion.7
  211.7 23.4 %subtract_reduce_fusion.2 = (f32[1024]{0:T(1024)S(1)}, f32[1024]{0:T(1024)S(1)}) fusion(f32[1024]{0:T(1024)S(1)} %bitcast.474, f32[1024]{0:T(1024)S(1)} %bitcast.477, f32[1024]{0:T(1024)S(1)} %bitcast.476, f32[1024]{0:T(1024)S(1)} %bitcast.475, f32[1024]{0:T(1024)S(1)} %bitcast.487, f32[1024]{0:T(1024)S(1)} %bitcast.490, f32[1024]{0:T(1024)S(1)} %bitcast.489, ...), kind=kLoop, calls=%fused_computation.22 | loop fusion | flops 52426752 | bytes 73732 | tf_op jit(solution)/shard_map/reduce_sum | solution.py:99
  235.1 23.4 %subtract_reduce_fusion.3 = (f32[1024]{0:T(1024)S(1)}, f32[1024]{0:T(1024)S(1)}) fusion(f32[1024]{0:T(1024)S(1)} %bitcast.457, f32[1024]{0:T(1024)S(1)} %bitcast.460, f32[1024]{0:T(1024)S(1)} %bitcast.459, f32[1024]{0:T(1024)S(1)} %bitcast.458, f32[1024]{0:T(1024)S(1)} %bitcast.480, f32[1024]{0:T(1024)S(1)} %bitcast.483, f32[1024]{0:T(1024)S(1)} %bitcast.482, ...), kind=kLoop, calls=%fused_computation.30 | loop fusion | flops 52426752 | bytes 73732 | tf_op jit(solution)/shard_map/reduce_sum | solution.py:99
  258.6 0.9 copy.304
  259.5 1.7 reshape.516
  261.2 0.0 reduce-scatter.7.cloned.1.call-update
  261.2 215.2 %reduce-scatter.7.cloned.1.call-done = f32[32,8]{1,0:T(8,128)} async-done(((f32[1024,8]{1,0:T(8,128)}), f32[32,8]{1,0:T(8,128)}) %reduce-scatter.7.cloned.1.call-update) | async-done | bytes 1040
  476.4 0.8 reshape.517
  477.2 0.7 copy.301
  (32 shorter events, 0.3 us)
Async XLA Ops:
  6.5 11.3 %copy-start.1 = (s32[2048]{0:T(1024)S(1)}, s32[2048]{0:T(1024)}, u32[]{:S(2)}) copy-start(s32[2048]{0:T(1024)} %param.9) | copy-start | bytes 24580
  6.5 19.5 %copy-start.3 = (f32[3,2048]{1,0:T(4,128)S(1)}, f32[3,2048]{1,0:T(4,128)}, u32[]{:S(2)}) copy-start(f32[3,2048]{1,0:T(4,128)} %param.7) | copy-start | bytes 73732
  6.5 19.6 %copy-start.2 = (f32[3,2048]{1,0:T(4,128)S(1)}, f32[3,2048]{1,0:T(4,128)}, u32[]{:S(2)}) copy-start(f32[3,2048]{1,0:T(4,128)} %param.6) | copy-start | bytes 73732
  17.8 26.8 %copy-start = (f32[32,5,2048]{2,0,1:T(8,128)S(1)}, f32[32,5,2048]{2,0,1:T(8,128)}, u32[]{:S(2)}) copy-start(f32[32,5,2048]{2,0,1:T(8,128)} %param.5) | copy-start | bytes 3932164
  33.2 25.1 %all-to-all-start = ((f32[32,1,448]{2,1,0:T(1,128)}), f32[32,1,448]{2,1,0:T(1,128)S(1)}, u32[]{:S(2)}, u32[]{:S(2)}) async-start(f32[32,1,448]{2,1,0:T(1,128)} %reshape.521), calls=%async_computation | async-start | bytes 131072 | tf_op jit(solution)/shard_map/all_to_all | solution.py:174
  58.3 59.5 %all-to-all-start.1 = ((f32[160,32,64]{0,2,1:T(8,128)}), f32[160,32,64]{0,2,1:T(8,128)S(1)}, u32[]{:S(2)}, u32[]{:S(2)}) async-start(f32[160,32,64]{0,2,1:T(8,128)} %broadcast_select_fusion), calls=%async_computation.1 | async-start | bytes 4194304 | tf_op jit(solution)/shard_map/all_to_all | solution.py:167
  68.1 88.0 %reduce-scatter.5.cloned.1.call-start = ((), (), s32[]{:S(2)}) async-start(), calls=%async_computation.4 | async-start | bytes 2359296 | tf_op jit(solution)/shard_map/reduce_scatter | solution.py:114
  123.3 2.5 copy-start.4
  125.5 350.9 %reduce-scatter.7.cloned.1.call-start = ((), (), s32[]{:S(2)}) async-start(), calls=%async_computation.5 | async-start | bytes 540672
Sparse Core Ops, SparseCore 0:
  125.6 30.4 reduce-scatter.4
  261.3 215.0 reduce-scatter.6
where the time goes:
time: 493 us; the launch traced here: 485 us
  waiting for transfers between devices  289 us (59%)
  other arithmetic  119 us (24%)
  local copies, waits for them, and re-layouts  40.1 us (8%)
  starting transfers between devices  21.5 us (4%)
  between operations  14.1 us (3%)
    unnamed x3, waiting for transfers between devices  215 us
    reduce_sum x4, other arithmetic, propagate(): jnp.sum(term_real, axis=1)  93.7 us
    all_to_all x1, waiting for transfers between devices, on_device(): lax.all_to_all(pack_rows(flat_series, source_of, groups, capacity), 'pane...  47.2 us
    reduce_scatter x1, waiting for transfers between devices, frequency_terms(): lax.psum_scatter(product.reshape(FREQ // lax.axis_size('obs') * lax.axis_...  26.8 us
    gather x3, local copies, waits for them, and re-layouts, pack_rows(): packed = jnp.take(values, source_of, axis=1, mode='fill', fill_value=0)  14.4 us
    all_to_all x1, starting transfers between devices, on_device(): lax.all_to_all(pack_rows(geometry, source_of, groups, capacity), 'panel',...  11.3 us
  transfers between devices with their start and end apart: 4, of which 3 were waited for; matrix products, arithmetic and copies ran while one was open for 4% of the time, Pallas kernels for 0%

commit v1 on v0

v1 whole, which is shorter than its diff:
```python
import math

import jax
import jax.numpy as jnp
import numpy as np
from jax import lax
from jax.experimental import pallas as pl
from jax.experimental.pallas import tpu as pltpu
from jax.sharding import PartitionSpec as P

TIME = 256
FREQ = 32
MACH_NUMBER = 0.3
SAMPLE_SPACING = 0.04
FOUR_PI = 4.0 * math.pi
BASE = 2.0 * math.pi / (TIME * SAMPLE_SPACING)

OBSERVERS = 1024
SLOTS = 2048
HALF = SLOTS // 2
STEPS = 32
CHIPS = 4
BAND = 8
LIST = 256
GROUP = 16
DEPTH = 128
MIB = 1 << 20

F32 = jnp.float32
BF16 = jnp.bfloat16


def sine_fits():
    node = np.cos((np.arange(400) + 0.5) * np.pi / 400) * 0.5 + 0.5
    square = node * 1.3**2
    angle = np.sqrt(square)
    table = []
    for values, degree in ((np.sin(angle) / angle, 5), (np.cos(angle), 6)):
        fit = np.polynomial.chebyshev.Chebyshev.fit(square, values, degree, domain=[0, 1.3**2])
        table.append([float(v) for v in fit.convert(kind=np.polynomial.Polynomial).coef])
    return table


SIN_FIT, COS_FIT = sine_fits()


def fourier_table():
    out = np.zeros((8, 64, 192), np.float32)
    high_out = np.zeros((8, 64, 192), np.float32)
    for block in range(8):
        chip, core = block // 2, block % 2
        for rel in range(CHIPS):
            band = (chip + rel) % CHIPS
            for part in range(2):
                for k in range(BAND):
                    row = (rel * 2 + part) * BAND + k
                    for source in range(2):
                        steps = 64 * chip + 32 * (core ^ source) + np.arange(STEPS)
                        turns = (BAND * band + k + 1) * steps % TIME
                        angle = turns * (2.0 * np.pi / TIME)
                        val = (np.cos(angle) if part == 0 else -np.sin(angle)) * (2.0 / TIME)
                        val = val.astype(np.float32)
                        high = val.astype(jnp.bfloat16).astype(np.float32)
                        low = (val - high).astype(np.float32)
                        lane = 32 * source
                        high_out[block, row, lane : lane + 32] = high
                        high_out[block, row, 64 + lane : 96 + lane] = high
                        high_out[block, row, 128 + lane : 160 + lane] = low
    return high_out.astype(jnp.bfloat16)


def params():
    return pltpu.CompilerParams(vmem_limit_bytes=56 * MIB)


def split(value):
    high = value.astype(BF16)
    low = (value - high.astype(F32)).astype(BF16)
    return high, low


def source_kernel(series_ref, area_ref, owner_ref, keep_ref, send_ref):
    core = lax.rem(lax.axis_index("obs"), 2)
    live = (owner_ref[...] >= 0).astype(F32)
    area = area_ref[...] * live
    a1, a2, a3 = area[0:1], area[1:2], area[2:3]
    convect = MACH_NUMBER * a1
    for pair in range(8):
        blocks = []
        for side in range(2):
            lanes = slice(128 * (2 * pair + side), 128 * (2 * pair + side) + 128)
            field = [series_ref[:, f, lanes] for f in range(5)]
            b1, b2, b3, bc = a1[:, lanes], a2[:, lanes], a3[:, lanes], convect[:, lanes]
            flux = b1 * field[1] + b2 * field[2] + b3 * field[3] + bc * field[0]
            blocks.append(
                [
                    flux,
                    b1 * field[4] + bc * field[1],
                    b2 * field[4] + bc * field[2],
                    b3 * field[4] + bc * field[3],
                ]
            )
        lanes = slice(128 * pair, 128 * pair + 128)
        for f in range(4):
            even, odd = blocks[0][f], blocks[1][f]
            rows = slice(32 * f, 32 * f + 32)
            keep_ref[rows, lanes] = jnp.where(core == 0, even, odd)
            send_ref[rows, lanes] = jnp.where(core == 0, odd, even)


def band_kernel(keep_ref, recv_ref, table_ref, own_ref, up_ref, down_ref, far_a_ref, far_b_ref):
    table = table_ref[lax.axis_index("obs")]
    for f in range(4):
        rows = slice(32 * f, 32 * f + 32)
        for tile in range(HALF // 256):
            lanes = slice(256 * tile, 256 * tile + 256)
            kh, kl = split(keep_ref[rows, lanes])
            rh, rl = split(recv_ref[rows, lanes])
            stack = jnp.concatenate([kh, rh, kl, rl, kh, rh], axis=0)
            part = jnp.dot(table, stack, preferred_element_type=F32)
            out = slice(HALF * f + 256 * tile, HALF * f + 256 * tile + 256)
            own_ref[:, out] = part[0:16]
            up_ref[:, out] = part[16:32]
            down_ref[:, out] = part[48:64]
            if f < 2:
                far_a_ref[:, out] = part[32:48]
            else:
                half = slice(out.start - 2 * HALF, out.stop - 2 * HALF)
                far_b_ref[:, half] = part[32:48]


def double(cosine, sine):
    twice = cosine + cosine
    return twice * cosine - 1.0, twice * sine


def geometry_kernel(pos_ref, obs_ref, r_ref, er_ref, ei_ref, gr_ref, gi_ref):
    place = lax.axis_index("obs")
    core = lax.rem(place, 2)
    chip = lax.div(place, 2)
    pos = jnp.where(core == 0, pos_ref[:, 0:128], pos_ref[:, 128:256])
    pos = jnp.concatenate([pos, jnp.zeros((5, 128), F32)], axis=0)
    pos = jnp.transpose(pos)

    def body(power):
        for g in range(16):
            rows = slice(8 * g, 8 * g + 8)
            y = [jnp.broadcast_to(pos[rows, i : i + 1], (8, 128)) for i in range(3)]
            for tile in range(LIST // 128):
                lanes = slice(128 * tile, 128 * tile + 128)
                square = None
                for i in range(3):
                    delta = obs_ref[i : i + 1, lanes] - y[i]
                    square = delta * delta if square is None else square + delta * delta
                inverse = lax.rsqrt(square)
                r = square * inverse
                half = r * (0.5 * BASE) - 0.5 * math.pi
                s2 = half * half
                sine = jnp.full_like(s2, SIN_FIT[-1])
                for c in SIN_FIT[-2::-1]:
                    sine = sine * s2 + c
                sine = sine * half
                cosine = jnp.full_like(s2, COS_FIT[-1])
                for c in COS_FIT[-2::-1]:
                    cosine = cosine * s2 + c
                twice = sine + sine
                er = twice * sine - 1.0
                ei = twice * cosine
                amp = inverse * inverse * inverse * (1.0 / FOUR_PI)
                if power == 0:
                    gr, gi = amp, jnp.zeros_like(amp)
                else:
                    cr, ci = er, ei
                    for _ in range(3):
                        cr, ci = double(cr, ci)
                    if power == 2:
                        cr, ci = double(cr, ci)
                    elif power == 3:
                        dr, di = double(cr, ci)
                        cr, ci = cr * dr - ci * di, cr * di + ci * dr
                    gr, gi = amp * cr, amp * ci
                r_ref[rows, lanes] = r
                er_ref[rows, lanes] = er
                ei_ref[rows, lanes] = ei
                gr_ref[rows, lanes] = gr
                gi_ref[rows, lanes] = gi

    for power in range(CHIPS):
        pl.when(chip == power)(lambda power=power: body(power))


def build_left(spec, pos_ref, wave_ref, stage, left):
    core = lax.rem(lax.axis_index("obs"), 2)
    first_band = lax.div(lax.axis_index("obs"), 2) * BAND
    wave = (lax.broadcasted_iota(jnp.int32, (BAND, 128), 0) + (first_band + 1)).astype(F32) * BASE
    left[...] = jnp.zeros(left.shape, BF16)

    def chunk(c, carry):
        lanes = pl.ds(pl.multiple_of(c * 128, 128), 128)
        wide = pl.multiple_of(c * 256, 256)
        y = jnp.where(
            core == 0, pos_ref[:, pl.ds(wide, 128)], pos_ref[:, pl.ds(wide + 128, 128)]
        )
        y = [y[i : i + 1] for i in range(3)]
        square = y[0] * y[0] + y[1] * y[1] + y[2] * y[2]
        flux = spec(0, c)
        load = [spec(1 + i, c) for i in range(3)]
        gains = (-wave * flux[1], wave * flux[0])
        moment = [
            -(y[0] * load[0][p] + y[1] * load[1][p] + y[2] * load[2][p]) for p in range(2)
        ]
        for p in range(2):
            g = gains[p]
            rows = [gains[p] * square + moment[p]]
            rows += [load[i][p] - 2.0 * (y[i] * g) for i in range(3)]
            rows += [g]
            for q in range(5):
                stage[p, 8 * q : 8 * q + 8, :] = rows[q]
            rows = [wave * moment[p]] + [wave * load[i][p] for i in range(3)]
            for q in range(4):
                stage[2 + p, 8 * q : 8 * q + 8, :] = rows[q]
            stage[2 + p, 32:40, :] = jnp.zeros((8, 128), F32)
        for comp in range(4):
            for k in range(BAND):
                rows = stage[comp, pl.ds(k, 8, stride=8), :]
                rows = jnp.concatenate(
                    [rows, jnp.zeros((120, 128), F32)], axis=0
                )
                turned = jnp.transpose(rows)[:, 0:8]
                high, low = split(turned)
                block = jnp.concatenate([high, low, high], axis=1).reshape(8, GROUP, 24)
                left[pl.ds(c * 8, 8), k * 4 + comp, :, 0:24] = block
        return carry

    lax.fori_loop(0, HALF // 128, chunk, 0)


def field_kernel(
    own_ref, up_ref, down_ref, pos_ref, feature_ref,
    r_ref, er_ref, ei_ref, gr_ref, gi_ref,
    out_ref, stage, left, result, total,
):
    tile, quarter = pl.program_id(0), pl.program_id(1)

    def spec(f, c):
        lanes = pl.ds(pl.multiple_of(HALF * f + c * 128, 128), 128)
        value = own_ref[:, lanes] + up_ref[:, lanes] + down_ref[:, lanes]
        return value[0:8], value[8:16]

    @pl.when(jnp.logical_and(tile == 0, quarter == 0))
    def _():
        stage[...] = jnp.zeros(stage.shape, F32)
        build_left(spec, pos_ref, None, stage, left)

    @pl.when(quarter == 0)
    def _():
        total[...] = jnp.zeros(total.shape, F32)

    groups = 16
    first = quarter * groups

    def product(g):
        lhs = left[g].reshape(32 * GROUP, DEPTH)
        return jnp.dot(lhs, feature_ref[...], preferred_element_type=F32)

    result[0] = product(first)

    def step(g, acc):
        now = lax.rem(g, 2)

        result[1 - now] = product(first + jnp.minimum(g + 1, groups - 1))
        acc = list(acc)
        for sub in range(2):
            rows = pl.ds(pl.multiple_of(g * GROUP + 8 * sub, 8), 8)
            for lane in range(2):
                lanes = slice(128 * lane, 128 * lane + 128)
                r = r_ref[rows, lanes]
                er, ei = er_ref[rows, lanes], ei_ref[rows, lanes]
                pr, pi = gr_ref[rows, lanes], gi_ref[rows, lanes]
                cr, ci = pr * er - pi * ei, pr * ei + pi * er
                twice = er + er
                for k in range(BAND):
                    base = k * 4 * GROUP + 8 * sub
                    m = [result[now, base + GROUP * c : base + GROUP * c + 8, lanes] for c in range(4)]
                    tr = m[0] - r * m[3]
                    ti = m[1] + r * m[2]
                    slot = lane * 16 + 2 * k
                    acc[slot] = acc[slot] + (cr * tr - ci * ti)
                    acc[slot + 1] = acc[slot + 1] + (cr * ti + ci * tr)
                    if k + 1 < BAND:
                        pr, pi, cr, ci = cr, ci, twice * cr - pr, twice * ci - pi
        return tuple(acc)

    zero = jnp.zeros((8, 128), F32)
    acc = lax.fori_loop(0, groups, step, (zero,) * 32)
    for i in range(32):
        total[i] = total[i] + acc[i]

    @pl.when(quarter == 3)
    def _():
        lane_block = lax.broadcasted_iota(jnp.int32, (4, 128), 1) // 32
        for lane in range(2):
            sums = [jnp.sum(total[lane * 16 + i], axis=0, keepdims=True) for i in range(16)]
            packs = [
                jnp.concatenate(
                    [sums[2 * kk], sums[2 * kk + 1], sums[2 * (4 + kk)], sums[2 * (4 + kk) + 1]],
                    axis=0,
                )
                for kk in range(4)
            ]
            for m in range(4):
                value = None
                for kk in range(4):
                    shift = (32 * (kk - m)) % 128
                    turned = pltpu.roll(packs[kk], shift, axis=1) if shift else packs[kk]
                    value = turned if value is None else jnp.where(lane_block == kk, turned, value)
                out_ref[4 * lane + m] = value


def finish_kernel(parts_ref, own_ref, send_ref):
    core = lax.rem(lax.axis_index("obs"), 2)
    value = jnp.sum(parts_ref[...], axis=0)
    own_ref[...] = jnp.where(core == 0, value[0:2], value[2:4])
    send_ref[...] = jnp.where(core == 0, value[2:4], value[0:2])


def shape(*dims, dtype=F32):
    return jax.ShapeDtypeStruct(dims, dtype)


def feature_kernel(observers_ref, out_ref):
    x = observers_ref[...]
    rows = jnp.concatenate(
        [
            jnp.ones((1, OBSERVERS), F32),
            x,
            x[0:1] * x[0:1] + x[1:2] * x[1:2] + x[2:3] * x[2:3],
            jnp.zeros((3, OBSERVERS), F32),
        ],
        axis=0,
    )
    high = rows.astype(BF16).astype(F32)
    low = rows - high
    rest = jnp.zeros((DEPTH - 24, OBSERVERS), F32)
    out_ref[...] = jnp.concatenate([high, high, low, rest], axis=0).astype(BF16)


def on_device(series, panel_pos, panel_area, observers, owner):
    whole = pl.BlockSpec(memory_space=pltpu.VMEM)
    keep, send = pl.pallas_call(
        source_kernel,
        out_shape=(shape(128, HALF), shape(128, HALF)),
        in_specs=[whole] * 3,
        out_specs=(whole, whole),
        compiler_params=params(),
        name="sources",
    )(series, panel_area, owner.reshape(1, SLOTS))
    swap = [(i, i ^ 1) for i in range(8)]
    above = [(i, (i + 2) % 8) for i in range(8)]
    below = [(i, (i + 6) % 8) for i in range(8)]
    recv = lax.ppermute(send, "obs", swap)

    pair_count = HALF * OBSERVERS
    block = pl.BlockSpec((128, LIST), lambda i, j: (i, j))
    geometry = pl.pallas_call(
        geometry_kernel,
        grid=(HALF // 128, OBSERVERS // LIST),
        out_shape=(shape(HALF, OBSERVERS),) * 5,
        in_specs=[
            pl.BlockSpec((3, 256), lambda i, j: (0, i)),
            pl.BlockSpec((3, LIST), lambda i, j: (0, j)),
        ],
        out_specs=(block,) * 5,
        compiler_params=params(),
        cost_estimate=pl.CostEstimate(
            flops=80 * pair_count, bytes_accessed=20 * pair_count, transcendentals=pair_count
        ),
        name="geometry",
    )(panel_pos, observers)

    own, up, down, far_a, far_b = pl.pallas_call(
        band_kernel,
        out_shape=(shape(16, 4 * HALF),) * 3 + (shape(16, 2 * HALF),) * 2,
        in_specs=[whole] * 3,
        out_specs=(whole,) * 5,
        compiler_params=params(),
        name="bands",
    )(keep, recv, jnp.asarray(fourier_table()))

    got_a = lax.ppermute(far_a, "obs", above)
    got_b = lax.ppermute(far_b, "obs", below)
    pad = jnp.zeros((16, 2 * HALF), F32)
    up = up + jnp.concatenate([got_a, pad], axis=1)
    down = down + jnp.concatenate([pad, got_b], axis=1)
    from_below = lax.ppermute(up, "obs", above)
    from_above = lax.ppermute(down, "obs", below)

    features = pl.pallas_call(
        feature_kernel,
        out_shape=shape(DEPTH, OBSERVERS, dtype=BF16),
        in_specs=[whole],
        out_specs=whole,
        compiler_params=params(),
        name="features",
    )(observers)
    quarter = HALF // 4
    near = pl.BlockSpec((quarter, LIST), lambda t, q: (q, t))
    chunks = pl.pallas_call(
        field_kernel,
        grid=(OBSERVERS // LIST, 4),
        out_shape=shape(32, 4, 128),
        in_specs=[whole] * 4 + [pl.BlockSpec((DEPTH, LIST), lambda t, q: (0, t))] + [near] * 5,
        out_specs=pl.BlockSpec((8, 4, 128), lambda t, q: (t, 0, 0)),
        scratch_shapes=[
            pltpu.VMEM((4, 64, 128), F32),
            pltpu.VMEM((HALF // GROUP, 32, GROUP, DEPTH), BF16),
            pltpu.VMEM((2, 32 * GROUP, LIST), F32),
            pltpu.VMEM((32, 8, 128), F32),
        ],
        compiler_params=params(),
        name="field",
    )(own, from_below, from_above, panel_pos, features, *geometry)

    parts = lax.all_to_all(chunks, "panel", split_axis=0, concat_axis=0, tiled=True)
    mine, other = pl.pallas_call(
        finish_kernel,
        out_shape=(shape(2, 128), shape(2, 128)),
        in_specs=[whole],
        out_specs=(whole, whole),
        compiler_params=params(),
        name="finish",
    )(parts)
    value = mine + lax.ppermute(other, "obs", swap)
    return jnp.transpose(value.reshape(2, 4, 32), (2, 0, 1))


def solution(mesh):
    in_specs = (P("obs", None, "panel"), P(None, "panel"), P(None, "panel"), P(), P("panel"))
    out_specs = P("panel", None, "obs")
    return jax.shard_map(
        on_device, mesh=mesh, in_specs=in_specs, out_specs=out_specs, check_vma=False
    )
```

time: 493 us -> 165 us (0.33)
  the two profiles are of different devices: /device:TPU:8 before, /device:TPU:25 now
where the time goes in v1:
time: 165 us; the launch traced here: 163 us
  Pallas kernels  119 us (72%)
  blocking collectives  20 us (12%)
  starting transfers between devices  9.36 us (6%)
  waiting for transfers between devices  6.24 us (4%)
  local copies, waits for them, and re-layouts  5.72 us (3%)
  other arithmetic  2.63 us (2%)
    pallas_call x1, Pallas kernels, on_device(): pl.pallas_call(field_kernel, grid=(OBSERVERS // LIST, 4), out_shape=shape...  87 us
    pallas_call x1, Pallas kernels, on_device(): pl.pallas_call(geometry_kernel, grid=(HALF // 128, OBSERVERS // LIST), ou...  23.4 us
    all_to_all x1, blocking collectives, on_device(): lax.all_to_all(chunks, 'panel', split_axis=0, concat_axis=0, tiled=True)  20 us
    unnamed x7, local copies, waits for them, and re-layouts  5.04 us
    ppermute x1, waiting for transfers between devices, on_device(): got_b = lax.ppermute(far_b, 'obs', below)  3.45 us
  transfers between devices with their start and end apart: 6, of which 3 were waited for; matrix products, arithmetic and copies ran while one was open for 1% of the time, Pallas kernels for 15%

profile of v1, /device:TPU:25, one launch (start us, length us, event | category | flops | bytes accessed | tf_op | source)
XLA Modules:
  0.0 163.1 jit_solution(854243323931981921)
XLA Ops:
  0.0 3.5 %copy.7.series_ref = f32[32,5,2048]{2,1,0:T(8,128)} copy(f32[32,5,2048]{2,0,1:T(8,128)} %param.6) | data formatting | bytes 2621440 | tf_op args[0]
  3.5 3.2 %sources.1 = (f32[128,1024]{1,0:T(8,128)}, f32[128,1024]{1,0:T(8,128)}) custom-call(f32[32,5,2048]{2,1,0:T(8,128)} %copy.7.series_ref, f32[3,2048]{1,0:T(4,128)} %area_ref.1, s32[1,2048]{1,0:T(1,128)} %bitcast.2), custom_call_target="tpu_custom_call" | custom-call | tf_op jit(solution)/shard_map/sources/pallas_call | solution.py:350
  6.6 0.7 collective-permute-start
  7.3 1.7 %collective-permute-done.recv_ref = f32[128,1024]{1,0:T(8,128)S(1)} collective-permute-done((f32[128,1024]{1,0:T(8,128)}, f32[128,1024]{1,0:T(8,128)S(1)}, u32[]{:S(2)}, u32[]{:S(2)}) %collective-permute-start) | collective-permute-done | bytes 524320 | tf_op jit(solution)/shard_map/ppermute | solution.py:361
  9.0 0.0 copy-start
  9.1 0.8 copy-done
  9.9 2.6 %bands.1 = (f32[16,4096]{1,0:T(8,128)}, f32[16,4096]{1,0:T(8,128)}, f32[16,4096]{1,0:T(8,128)}, f32[16,2048]{1,0:T(8,128)}, f32[16,2048]{1,0:T(8,128)}) custom-call(f32[128,1024]{1,0:T(8,128)} %get-tuple-element.19.keep_ref, f32[128,1024]{1,0:T(8,128)} %copy-done, bf16[8,64,192]{2,1,0:T(8,128)(2,1)} %constant.4.clone.table_ref), custom_call_target="tpu_custom_call" | custom-call | tf_op jit(solution)/shard_map/bands/pallas_call | solution.py:381
  12.5 0.5 collective-permute-start.3
  12.9 2.2 %collective-permute-start.1 = (f32[16,2048]{1,0:T(8,128)}, f32[16,2048]{1,0:T(8,128)S(1)}, u32[]{:S(2)}, u32[]{:S(2)}) collective-permute-start(f32[16,2048]{1,0:T(8,128)} %get-tuple-element.23), channel_id=1, source_target_pairs={{0,2},{1,3},{2,4},{3,5},{4,6},{5,7},{6,0},{7,1},{8,10},{9,11},{10,... | collective-permute-start | bytes 393224 | tf_op jit(solution)/shard_map/ppermute | solution.py:390
  15.1 3.5 %collective-permute-done.3 = f32[16,2048]{1,0:T(8,128)S(1)} collective-permute-done((f32[16,2048]{1,0:T(8,128)}, f32[16,2048]{1,0:T(8,128)S(1)}, u32[]{:S(2)}, u32[]{:S(2)}) %collective-permute-start.3) | collective-permute-done | bytes 131104 | tf_op jit(solution)/shard_map/ppermute | solution.py:391
  18.6 1.0 pad_add_fusion
  19.6 0.1 collective-permute-start.4
  19.7 0.0 collective-permute-done.1
  19.7 1.0 pad_add_fusion.1
  20.6 2.7 %collective-permute-start.2 = (f32[16,4096]{1,0:T(8,128)S(1)}, f32[16,4096]{1,0:T(8,128)S(1)}, u32[]{:S(2)}, u32[]{:S(2)}) collective-permute-start(f32[16,4096]{1,0:T(8,128)S(1)} %pad_add_fusion.1), channel_id=1, source_target_pairs={{0,2},{1,3},{2,4},{3,5},{4,6},{5,7},{6,0},{7,1},{8,10},{9,11},{10,... | collective-permute-start | bytes 786440 | tf_op jit(solution)/shard_map/ppermute | solution.py:395
  23.4 1.4 features.1.feature_ref
  24.8 23.4 %geometry.1 = (f32[1024,1024]{1,0:T(8,128)}, f32[1024,1024]{1,0:T(8,128)}, f32[1024,1024]{1,0:T(8,128)}, f32[1024,1024]{1,0:T(8,128)}, f32[1024,1024]{1,0:T(8,128)}) custom-call(f32[3,2048]{1,0:T(4,128)} %pos_ref.3, f32[3,1024]{1,0:T(4,128)} %obs_ref.1), custom_call_target="tpu_custom_call" | custom-call | flops 83886080 | bytes 20971520 | tf_op jit(solution)/shard_map/geometry/pallas_call | solution.py:365
  48.2 0.0 collective-permute-done.4.down_ref
  48.2 0.0 copy-start.1
  48.2 0.0 collective-permute-done.2.up_ref
  48.2 0.0 copy-start.2
  48.3 0.7 copy-done.1
  49.0 0.1 copy-done.2
  49.0 87.0 %field.1 = f32[32,4,128]{2,1,0:T(4,128)} custom-call(f32[16,4096]{1,0:T(8,128)} %get-tuple-element.21.own_ref, f32[16,4096]{1,0:T(8,128)} %copy-done.2, f32[16,4096]{1,0:T(8,128)} %copy-done.1, f32[3,2048]{1,0:T(4,128)} %pos_ref.3, bf16[128,1024]{1,0:T(8,128)(2,1)} %features.1.feature_ref, f32[1024,1024]{1,0:T(8,128)} %get-tuple-element.26.r_ref, ...), custom_call_target="tpu_custom_call" | custom-call | tf_op jit(solution)/shard_map/field/pallas_call | solution.py:408
  136.1 20.0 %all_to_all.5.parts_ref = f32[32,4,128]{2,1,0:T(4,128)} all-to-all(f32[32,4,128]{2,1,0:T(4,128)} %field.1), channel_id=1, replica_groups=mesh['panel'=32,'obs'=8] {'panel'}, dimensions={0} | all-to-all | bytes 131072 | tf_op jit(solution)/shard_map/all_to_all | solution.py:424
  156.1 1.5 finish.1
  157.5 3.2 %collective-permute-start.5 = (f32[2,128]{1,0:T(2,128)}, f32[2,128]{1,0:T(2,128)S(1)}, u32[]{:S(2)}, u32[]{:S(2)}) collective-permute-start(f32[2,128]{1,0:T(2,128)} %get-tuple-element.32), channel_id=1, source_target_pairs={{0,1},{1,0},{2,3},{3,2},{4,5},{5,4},{6,7},{7,6},{8,9},{9,8},{10,11... | collective-permute-start | bytes 3080 | tf_op jit(solution)/shard_map/ppermute | solution.py:433
  160.7 1.0 collective-permute-done.5
  161.7 0.7 add.15
  162.4 0.7 reshape.7
Async XLA Ops:
  6.6 2.4 %collective-permute-start = (f32[128,1024]{1,0:T(8,128)}, f32[128,1024]{1,0:T(8,128)S(1)}, u32[]{:S(2)}, u32[]{:S(2)}) collective-permute-start(f32[128,1024]{1,0:T(8,128)} %get-tuple-element.20), channel_id=1, source_target_pairs={{0,1},{1,0},{2,3},{3,2},{4,5},{5,4},{6,7},{7,6},{8,9},{9,8},{10,11... | collective-permute-start | bytes 1572872 | tf_op jit(solution)/shard_map/ppermute | solution.py:361
  9.0 0.8 copy-start
  12.5 6.1 %collective-permute-start.3 = (f32[16,2048]{1,0:T(8,128)}, f32[16,2048]{1,0:T(8,128)S(1)}, u32[]{:S(2)}, u32[]{:S(2)}) collective-permute-start(f32[16,2048]{1,0:T(8,128)} %get-tuple-element.25), channel_id=1, source_target_pairs={{0,6},{1,7},{2,0},{3,1},{4,2},{5,3},{6,4},{7,5},{8,14},{9,15},{10,... | collective-permute-start | bytes 393224 | tf_op jit(solution)/shard_map/ppermute | solution.py:391
  12.9 6.7 %collective-permute-start.1 = (f32[16,2048]{1,0:T(8,128)}, f32[16,2048]{1,0:T(8,128)S(1)}, u32[]{:S(2)}, u32[]{:S(2)}) collective-permute-start(f32[16,2048]{1,0:T(8,128)} %get-tuple-element.23), channel_id=1, source_target_pairs={{0,2},{1,3},{2,4},{3,5},{4,6},{5,7},{6,0},{7,1},{8,10},{9,11},{10,... | collective-permute-start | bytes 393224 | tf_op jit(solution)/shard_map/ppermute | solution.py:390
  19.6 28.7 %collective-permute-start.4 = (f32[16,4096]{1,0:T(8,128)S(1)}, f32[16,4096]{1,0:T(8,128)S(1)}, u32[]{:S(2)}, u32[]{:S(2)}) collective-permute-start(f32[16,4096]{1,0:T(8,128)S(1)} %pad_add_fusion), channel_id=1, source_target_pairs={{0,6},{1,7},{2,0},{3,1},{4,2},{5,3},{6,4},{7,5},{8,14},{9,15},{10,... | collective-permute-start | bytes 786440 | tf_op jit(solution)/shard_map/ppermute | solution.py:396
  20.6 27.6 %collective-permute-start.2 = (f32[16,4096]{1,0:T(8,128)S(1)}, f32[16,4096]{1,0:T(8,128)S(1)}, u32[]{:S(2)}, u32[]{:S(2)}) collective-permute-start(f32[16,4096]{1,0:T(8,128)S(1)} %pad_add_fusion.1), channel_id=1, source_target_pairs={{0,2},{1,3},{2,4},{3,5},{4,6},{5,7},{6,0},{7,1},{8,10},{9,11},{10,... | collective-permute-start | bytes 786440 | tf_op jit(solution)/shard_map/ppermute | solution.py:395
  48.2 0.7 copy-start.1
  48.2 0.8 copy-start.2
  157.5 4.2 %collective-permute-start.5 = (f32[2,128]{1,0:T(2,128)}, f32[2,128]{1,0:T(2,128)S(1)}, u32[]{:S(2)}, u32[]{:S(2)}) collective-permute-start(f32[2,128]{1,0:T(2,128)} %get-tuple-element.32), channel_id=1, source_target_pairs={{0,1},{1,0},{2,3},{3,2},{4,5},{5,4},{6,7},{7,6},{8,9},{9,8},{10,11... | collective-permute-start | bytes 3080 | tf_op jit(solution)/shard_map/ppermute | solution.py:433

commit v2 on v1

v2 whole, which is shorter than its diff:
```python
import math

import jax
import jax.numpy as jnp
import numpy as np
from jax import lax
from jax.experimental import pallas as pl
from jax.experimental.pallas import tpu as pltpu
from jax.sharding import PartitionSpec as P

TIME = 256
FREQ = 32
MACH_NUMBER = 0.3
SAMPLE_SPACING = 0.04
FOUR_PI = 4.0 * math.pi
BASE = 2.0 * math.pi / (TIME * SAMPLE_SPACING)

OBSERVERS = 1024
SLOTS = 2048
HALF = SLOTS // 2
STEPS = 32
CHIPS = 4
BAND = 8
LIST = 256
GROUP = 16
BATCH = 128
PIECES = 8
DEPTH = 128
MIB = 1 << 20

F32 = jnp.float32
BF16 = jnp.bfloat16


def sine_fits():
    node = np.cos((np.arange(400) + 0.5) * np.pi / 400) * 0.5 + 0.5
    square = node * 1.3**2
    angle = np.sqrt(square)
    table = []
    for values, degree in ((np.sin(angle) / angle, 5), (np.cos(angle), 6)):
        fit = np.polynomial.chebyshev.Chebyshev.fit(square, values, degree, domain=[0, 1.3**2])
        table.append([float(v) for v in fit.convert(kind=np.polynomial.Polynomial).coef])
    return table


SIN_FIT, COS_FIT = sine_fits()


def fourier_table():
    out = np.zeros((8, 64, 192), np.float32)
    high_out = np.zeros((8, 64, 192), np.float32)
    for block in range(8):
        chip, core = block // 2, block % 2
        for rel in range(CHIPS):
            band = (chip + rel) % CHIPS
            for part in range(2):
                for k in range(BAND):
                    row = (rel * 2 + part) * BAND + k
                    for source in range(2):
                        steps = 64 * chip + 32 * (core ^ source) + np.arange(STEPS)
                        turns = (BAND * band + k + 1) * steps % TIME
                        angle = turns * (2.0 * np.pi / TIME)
                        val = (np.cos(angle) if part == 0 else -np.sin(angle)) * (2.0 / TIME)
                        val = val.astype(np.float32)
                        high = val.astype(jnp.bfloat16).astype(np.float32)
                        low = (val - high).astype(np.float32)
                        lane = 32 * source
                        high_out[block, row, lane : lane + 32] = high
                        high_out[block, row, 64 + lane : 96 + lane] = high
                        high_out[block, row, 128 + lane : 160 + lane] = low
    return high_out.astype(jnp.bfloat16)


def params(mib=16):
    return pltpu.CompilerParams(vmem_limit_bytes=mib * MIB)


def split(value):
    high = value.astype(BF16)
    low = (value - high.astype(F32)).astype(BF16)
    return high, low


def source_kernel(series_ref, area_ref, owner_ref, keep_ref, send_ref):
    core = lax.rem(lax.axis_index("obs"), 2)
    live = (owner_ref[...] >= 0).astype(F32)
    area = area_ref[...] * live
    blocks = []
    for side in range(2):
        lanes = slice(128 * side, 128 * side + 128)
        field = [series_ref[:, f, lanes] for f in range(5)]
        b1, b2, b3 = area[0:1, lanes], area[1:2, lanes], area[2:3, lanes]
        bc = MACH_NUMBER * b1
        flux = b1 * field[1] + b2 * field[2] + b3 * field[3] + bc * field[0]
        blocks.append([flux] + [b * field[4] + bc * field[1 + i] for i, b in enumerate((b1, b2, b3))])
    for f in range(4):
        even, odd = blocks[0][f], blocks[1][f]
        rows = slice(32 * f, 32 * f + 32)
        keep_ref[rows, :] = jnp.where(core == 0, even, odd)
        send_ref[rows, :] = jnp.where(core == 0, odd, even)


def band_kernel(keep_ref, recv_ref, table_ref, own_ref, up_ref, down_ref, far_a_ref, far_b_ref):
    table = table_ref[lax.axis_index("obs")]
    for f in range(4):
        rows = slice(32 * f, 32 * f + 32)
        for tile in range(HALF // 256):
            lanes = slice(256 * tile, 256 * tile + 256)
            kh, kl = split(keep_ref[rows, lanes])
            rh, rl = split(recv_ref[rows, lanes])
            stack = jnp.concatenate([kh, rh, kl, rl, kh, rh], axis=0)
            part = jnp.dot(table, stack, preferred_element_type=F32)
            out = slice(HALF * f + 256 * tile, HALF * f + 256 * tile + 256)
            own_ref[:, out] = part[0:16]
            up_ref[:, out] = part[16:32]
            down_ref[:, out] = part[48:64]
            if f < 2:
                far_a_ref[:, out] = part[32:48]
            else:
                half = slice(out.start - 2 * HALF, out.stop - 2 * HALF)
                far_b_ref[:, half] = part[32:48]


def double(cosine, sine):
    twice = cosine + cosine
    return twice * cosine - 1.0, twice * sine


def geometry_kernel(pos_ref, obs_ref, r_ref, er_ref, ei_ref, gr_ref, gi_ref):
    place = lax.axis_index("obs")
    core = lax.rem(place, 2)
    chip = lax.div(place, 2)

    def tile_step(power, y, first, t):
        lanes = pl.ds(pl.multiple_of(t * 128, 128), 128)
        x = [jnp.broadcast_to(obs_ref[i : i + 1, lanes], (8, 128)) for i in range(3)]
        for g in range(16):
            rows = pl.ds(pl.multiple_of(first + 8 * g, 8), 8)
            square = None
            for i in range(3):
                delta = x[i] - jnp.broadcast_to(y[8 * g : 8 * g + 8, i : i + 1], (8, 128))
                square = delta * delta if square is None else square + delta * delta
            inverse = lax.rsqrt(square)
            r = square * inverse
            half = r * (0.5 * BASE) - 0.5 * math.pi
            s2 = half * half
            sine = s2 * SIN_FIT[-1] + SIN_FIT[-2]
            for c in SIN_FIT[-3::-1]:
                sine = sine * s2 + c
            sine = sine * half
            cosine = s2 * COS_FIT[-1] + COS_FIT[-2]
            for c in COS_FIT[-3::-1]:
                cosine = cosine * s2 + c
            twice = sine + sine
            er = twice * sine - 1.0
            ei = twice * cosine
            amp = inverse * inverse * (inverse * (1.0 / FOUR_PI))
            if power == 0:
                gr, gi = amp, jnp.zeros_like(amp)
            else:
                cr, ci = er, ei
                for _ in range(3):
                    cr, ci = double(cr, ci)
                if power == 2:
                    cr, ci = double(cr, ci)
                elif power == 3:
                    dr, di = double(cr, ci)
                    cr, ci = cr * dr - ci * di, cr * di + ci * dr
                gr, gi = amp * cr, amp * ci
            r_ref[rows, lanes] = r
            er_ref[rows, lanes] = er
            ei_ref[rows, lanes] = ei
            gr_ref[rows, lanes] = gr
            gi_ref[rows, lanes] = gi

    def body(power):
        def chunk(c, carry):
            wide = pl.multiple_of(c * 256, 256)
            pos = jnp.where(
                core == 0, pos_ref[:, pl.ds(wide, 128)], pos_ref[:, pl.ds(wide + 128, 128)]
            )
            pos = jnp.concatenate([pos, jnp.zeros((5, 128), F32)], axis=0)
            y = jnp.transpose(pos)

            def tile(t, inner):
                tile_step(power, y, c * 128, t)
                return inner

            lax.fori_loop(0, OBSERVERS // 128, tile, 0)
            return carry

        lax.fori_loop(0, HALF // 128, chunk, 0)

    for power in range(CHIPS):
        pl.when(chip == power)(lambda power=power: body(power))


def build_left(spec, pos_ref, stage, left):
    core = lax.rem(lax.axis_index("obs"), 2)
    first_band = lax.div(lax.axis_index("obs"), 2) * BAND
    wave = (lax.broadcasted_iota(jnp.int32, (BAND, 128), 0) + (first_band + 1)).astype(F32) * BASE
    freq_of = lax.broadcasted_iota(jnp.int32, (128, 128), 1) // 16
    stage[...] = jnp.zeros(stage.shape, F32)

    def chunk(c, carry):
        wide = pl.multiple_of(c * 256, 256)
        y = jnp.where(
            core == 0, pos_ref[:, pl.ds(wide, 128)], pos_ref[:, pl.ds(wide + 128, 128)]
        )
        y = [y[i : i + 1] for i in range(3)]
        square = y[0] * y[0] + y[1] * y[1] + y[2] * y[2]
        flux = spec(0, c)
        load = [spec(1 + i, c) for i in range(3)]
        gains = (-wave * flux[1], wave * flux[0])
        moment = [
            -(y[0] * load[0][p] + y[1] * load[1][p] + y[2] * load[2][p]) for p in range(2)
        ]
        comps = []
        for p in range(2):
            g = gains[p]
            rows = [g * square + moment[p]]
            rows += [load[i][p] - 2.0 * (y[i] * g) for i in range(3)]
            comps.append(rows + [g])
        for p in range(2):
            comps.append([wave * moment[p]] + [wave * load[i][p] for i in range(3)])
        for comp, rows in enumerate(comps):
            for q, row in enumerate(rows):
                high = row.astype(BF16).astype(F32)
                for place, value in ((q, high), (5 + q, row - high), (10 + q, high)):
                    stage[pl.ds(128 * comp + place, 8, stride=16), :] = value
        for comp in range(4):
            turned = jnp.transpose(stage[128 * comp : 128 * comp + 128, :])
            for k in range(BAND):
                block = jnp.where(freq_of == k, turned, 0.0).astype(BF16)
                left[pl.ds(c * 8, 8), comp * BAND + k] = block.reshape(8, GROUP, DEPTH)
        return carry

    lax.fori_loop(0, HALF // 128, chunk, 0)


def field_kernel(
    own_ref, up_ref, down_ref, pos_ref, feature_ref,
    r_ref, er_ref, ei_ref, gr_ref, gi_ref,
    out_ref, stage, left, ready, after, total,
):
    def spec(f, c):
        lanes = pl.ds(pl.multiple_of(HALF * f + c * 128, 128), 128)
        value = own_ref[:, lanes] + up_ref[:, lanes] + down_ref[:, lanes]
        return value[0:8], value[8:16]

    build_left(spec, pos_ref, stage, left)
    total[...] = jnp.zeros(total.shape, F32)
    batches = HALF // BATCH
    steps = batches * (OBSERVERS // LIST)
    groups = BATCH // GROUP

    def product(target, i, part):
        t, b = lax.div(i, batches), lax.rem(i, batches)
        size = 32 * GROUP * groups // PIECES
        if PIECES <= groups:
            lhs = left[pl.ds(b * groups + part * (groups // PIECES), groups // PIECES)]
        else:
            cut = PIECES // groups
            span = 32 // cut
            lhs = left[b * groups + part // cut, span * (part % cut) : span * (part % cut) + span]
        rhs = feature_ref[:, pl.ds(pl.multiple_of(t * LIST, LIST), LIST)]
        target[part * size : part * size + size] = jnp.dot(
            lhs.reshape(size, DEPTH), rhs, preferred_element_type=F32
        )

    def consume(source, i, target, following):
        t, b = lax.div(i, batches), lax.rem(i, batches)
        for lane in range(LIST // 128):
            lanes = pl.ds(pl.multiple_of(t * LIST + 128 * lane, 128), 128)
            near = slice(128 * lane, 128 * lane + 128)
            acc = [total[t, lane * 16 + i] for i in range(16)]
            for sub in range(BATCH // 8):
                piece, rest = divmod((lane * (BATCH // 8) + sub) * PIECES, BATCH // 4)
                if rest == 0:
                    product(target, following, piece)
                rows = pl.ds(pl.multiple_of(b * BATCH + 8 * sub, 8), 8)
                r = r_ref[rows, lanes]
                er, ei = er_ref[rows, lanes], ei_ref[rows, lanes]
                pr, pi = gr_ref[rows, lanes], gi_ref[rows, lanes]
                cr, ci = pr * er - pi * ei, pr * ei + pi * er
                twice = er + er
                for k in range(BAND):
                    m = []
                    for comp in range(4):
                        base = ((sub // 2) * 32 + comp * BAND + k) * GROUP + 8 * (sub % 2)
                        m.append(source[base : base + 8, near])
                    tr = m[0] - r * m[3]
                    ti = m[1] + r * m[2]
                    acc[2 * k] = acc[2 * k] + (cr * tr - ci * ti)
                    acc[2 * k + 1] = acc[2 * k + 1] + (cr * ti + ci * tr)
                    if k + 1 < BAND:
                        pr, pi, cr, ci = cr, ci, twice * cr - pr, twice * ci - pi
            for i in range(16):
                total[t, lane * 16 + i] = acc[i]

    for part in range(PIECES):
        product(ready, 0, part)

    def step(i, carry):
        following = jnp.minimum(i + 1, steps - 1)

        @pl.when(lax.rem(i, 2) == 0)
        def _():
            consume(ready, i, after, following)

        @pl.when(lax.rem(i, 2) == 1)
        def _():
            consume(after, i, ready, following)

        return carry

    lax.fori_loop(0, steps, step, 0)

    lane_block = lax.broadcasted_iota(jnp.int32, (4, 128), 1) // 32
    for t in range(OBSERVERS // LIST):
        for lane in range(LIST // 128):
            sums = [jnp.sum(total[t, lane * 16 + i], axis=0, keepdims=True) for i in range(16)]
            packs = [
                jnp.concatenate(
                    [sums[2 * kk], sums[2 * kk + 1], sums[2 * (4 + kk)], sums[2 * (4 + kk) + 1]],
                    axis=0,
                )
                for kk in range(4)
            ]
            for m in range(4):
                value = None
                for kk in range(4):
                    shift = (32 * (kk - m)) % 128
                    turned = pltpu.roll(packs[kk], shift, axis=1) if shift else packs[kk]
                    value = turned if value is None else jnp.where(lane_block == kk, turned, value)
                out_ref[8 * t + 4 * lane + m] = value


def finish_kernel(parts_ref, own_ref, send_ref):
    core = lax.rem(lax.axis_index("obs"), 2)
    value = jnp.sum(parts_ref[...], axis=0)
    own_ref[...] = jnp.where(core == 0, value[0:2], value[2:4])
    send_ref[...] = jnp.where(core == 0, value[2:4], value[0:2])


def shape(*dims, dtype=F32):
    return jax.ShapeDtypeStruct(dims, dtype)


def feature_kernel(observers_ref, out_ref):
    x = observers_ref[...]
    rows = jnp.concatenate(
        [
            jnp.ones((1, OBSERVERS), F32),
            x,
            x[0:1] * x[0:1] + x[1:2] * x[1:2] + x[2:3] * x[2:3],
        ],
        axis=0,
    )
    high = rows.astype(BF16).astype(F32)
    low = rows - high
    rest = jnp.zeros((1, OBSERVERS), F32)
    out_ref[...] = jnp.concatenate([high, high, low, rest] * BAND, axis=0).astype(BF16)


def on_device(series, panel_pos, panel_area, observers, owner):
    whole = pl.BlockSpec(memory_space=pltpu.VMEM)
    pair = pl.BlockSpec((128, 128), lambda i: (0, i))
    keep, send = pl.pallas_call(
        source_kernel,
        grid=(HALF // 128,),
        out_shape=(shape(128, HALF), shape(128, HALF)),
        in_specs=[
            pl.BlockSpec((STEPS, 5, 256), lambda i: (0, 0, i)),
            pl.BlockSpec((3, 256), lambda i: (0, i)),
            pl.BlockSpec((1, 256), lambda i: (0, i)),
        ],
        out_specs=(pair, pair),
        compiler_params=params(),
        name="sources",
    )(series, panel_area, owner.reshape(1, SLOTS))
    swap = [(i, i ^ 1) for i in range(8)]
    above = [(i, (i + 2) % 8) for i in range(8)]
    below = [(i, (i + 6) % 8) for i in range(8)]
    recv = lax.ppermute(send, "obs", swap)

    pair_count = HALF * OBSERVERS
    geometry = pl.pallas_call(
        geometry_kernel,
        out_shape=(shape(HALF, OBSERVERS),) * 5,
        in_specs=[whole] * 2,
        out_specs=(whole,) * 5,
        compiler_params=params(),
        cost_estimate=pl.CostEstimate(
            flops=80 * pair_count, bytes_accessed=20 * pair_count, transcendentals=pair_count
        ),
        name="geometry",
    )(panel_pos, observers)

    own, up, down, far_a, far_b = pl.pallas_call(
        band_kernel,
        out_shape=(shape(16, 4 * HALF),) * 3 + (shape(16, 2 * HALF),) * 2,
        in_specs=[whole] * 3,
        out_specs=(whole,) * 5,
        compiler_params=params(),
        name="bands",
    )(keep, recv, jnp.asarray(fourier_table()))

    got_a = lax.ppermute(far_a, "obs", above)
    got_b = lax.ppermute(far_b, "obs", below)
    pad = jnp.zeros((16, 2 * HALF), F32)
    up = up + jnp.concatenate([got_a, pad], axis=1)
    down = down + jnp.concatenate([pad, got_b], axis=1)
    from_below = lax.ppermute(up, "obs", above)
    from_above = lax.ppermute(down, "obs", below)

    features = pl.pallas_call(
        feature_kernel,
        out_shape=shape(DEPTH, OBSERVERS, dtype=BF16),
        in_specs=[whole],
        out_specs=whole,
        compiler_params=params(),
        name="features",
    )(observers)
    chunks = pl.pallas_call(
        field_kernel,
        out_shape=shape(32, 4, 128),
        in_specs=[whole] * 10,
        out_specs=whole,
        scratch_shapes=[
            pltpu.VMEM((512, 128), F32),
            pltpu.VMEM((HALF // GROUP, 32, GROUP, DEPTH), BF16),
            pltpu.VMEM((32 * BATCH, LIST), F32),
            pltpu.VMEM((32 * BATCH, LIST), F32),
            pltpu.VMEM((OBSERVERS // LIST, 32, 8, 128), F32),
        ],
        compiler_params=params(24),
        name="field",
    )(own, from_below, from_above, panel_pos, features, *geometry)

    parts = lax.all_to_all(chunks, "panel", split_axis=0, concat_axis=0, tiled=True)
    mine, other = pl.pallas_call(
        finish_kernel,
        out_shape=(shape(2, 128), shape(2, 128)),
        in_specs=[whole],
        out_specs=(whole, whole),
        compiler_params=params(),
        name="finish",
    )(parts)
    value = mine + lax.ppermute(other, "obs", swap)
    return jnp.transpose(value.reshape(2, 4, 32), (2, 0, 1))


def solution(mesh):
    in_specs = (P("obs", None, "panel"), P(None, "panel"), P(None, "panel"), P(), P("panel"))
    out_specs = P("panel", None, "obs")
    return jax.shard_map(
        on_device, mesh=mesh, in_specs=in_specs, out_specs=out_specs, check_vma=False
    )
```

time: 165 us -> 88.4 us (0.54); the launches traced: 163 us -> 88.2 us
  Pallas kernels: 119 us -> 48.8 us
  other arithmetic: 2.63 us -> 0.06 us
    pallas_call x3, Pallas kernels: 114 us -> 48.3 us  [the longest x1 30.6 us: on_device(): pl.pallas_call(field_kernel, out_shape=shape(32, 4, 128), in_specs=[whole...]
    pallas_call x1, Pallas kernels: 2.6 us -> 0.41 us  [on_device(): pl.pallas_call(band_kernel, out_shape=(shape(16, 4 * HALF),) * 3 + (shape...]
    unnamed x7 -> x11, local copies, waits for them, and re-layouts: 5.04 us -> 3.63 us
  transfers between devices with their start and end apart: 6 -> 6, of which waited for: 3 -> 3; matrix products, arithmetic and copies ran while one was open for 1% -> 0% of each run, Pallas kernels for 15% -> 19%
where the time goes in v2:
time: 88.4 us; the launch traced here: 88.2 us
  Pallas kernels  48.8 us (55%)
  blocking collectives  19.7 us (22%)
  starting transfers between devices  9.59 us (11%)
  waiting for transfers between devices  5.61 us (6%)
  local copies, waits for them, and re-layouts  4.31 us (5%)
    pallas_call x1, Pallas kernels, on_device(): pl.pallas_call(field_kernel, out_shape=shape(32, 4, 128), in_specs=[whole...  30.6 us
    all_to_all x1, blocking collectives, on_device(): lax.all_to_all(chunks, 'panel', split_axis=0, concat_axis=0, tiled=True)  19.7 us
    pallas_call x1, Pallas kernels, on_device(): pl.pallas_call(geometry_kernel, out_shape=(shape(HALF, OBSERVERS),) * 5,...  16.8 us
    unnamed x11, local copies, waits for them, and re-layouts  3.63 us
    ppermute x1, starting transfers between devices, on_device(): value = mine + lax.ppermute(other, 'obs', swap)  3.26 us
    ppermute x1, waiting for transfers between devices, on_device(): got_b = lax.ppermute(far_b, 'obs', below)  3.24 us
    ppermute x1, starting transfers between devices, on_device(): from_below = lax.ppermute(up, 'obs', above)  2.73 us
    ppermute x1, starting transfers between devices, on_device(): got_a = lax.ppermute(far_a, 'obs', above)  2.21 us
  transfers between devices with their start and end apart: 6, of which 3 were waited for; matrix products, arithmetic and copies ran while one was open for 0% of the time, Pallas kernels for 19%

profile of v2, /device:TPU:25, one launch (start us, length us, event | category | flops | bytes accessed | tf_op | source)
XLA Modules:
  0.0 88.2 jit_solution(4867249854541103858)
XLA Ops:
  0.0 0.0 copy-start
  0.0 0.0 copy-start.3
  0.0 0.0 copy-start.2
  0.0 2.2 %copy.7.series_ref = f32[32,5,2048]{2,1,0:T(8,128)S(1)} copy(f32[32,5,2048]{2,0,1:T(8,128)} %param.6) | data formatting | bytes 2621440 | tf_op args[0]
  2.2 0.0 copy-start.1
  2.2 0.7 copy-done.1
  2.9 0.0 copy-start.4
  2.9 0.7 copy-done.4
  3.6 0.9 %sources.1 = (f32[128,1024]{1,0:T(8,128)S(1)}, f32[128,1024]{1,0:T(8,128)S(1)}) custom-call(f32[32,5,2048]{2,1,0:T(8,128)S(1)} %copy.7.series_ref, f32[3,2048]{1,0:T(4,128)S(1)} %copy-done.1, s32[1,2048]{1,0:T(1,128)S(1)} %bitcast.2), custom_call_target="tpu_custom_call" | custom-call | tf_op jit(solution)/shard_map/sources/pallas_call | solution.py:369
  4.6 0.8 collective-permute-start
  5.4 1.5 %collective-permute-done.recv_ref = f32[128,1024]{1,0:T(8,128)S(1)} collective-permute-done((f32[128,1024]{1,0:T(8,128)S(1)}, f32[128,1024]{1,0:T(8,128)S(1)}, u32[]{:S(2)}, u32[]{:S(2)}) %collective-permute-start) | collective-permute-done | bytes 524320 | tf_op jit(solution)/shard_map/ppermute | solution.py:385
  6.9 0.0 copy-done
  6.9 0.4 bands.1
  7.3 0.5 collective-permute-start.3
  7.8 2.2 %collective-permute-start.1 = (f32[16,2048]{1,0:T(8,128)S(1)}, f32[16,2048]{1,0:T(8,128)S(1)}, u32[]{:S(2)}, u32[]{:S(2)}) collective-permute-start(f32[16,2048]{1,0:T(8,128)S(1)} %get-tuple-element.23), channel_id=1, source_target_pairs={{0,2},{1,3},{2,4},{3,5},{4,6},{5,7},{6,0},{7,1},{8,10},{9,11},{10,... | collective-permute-start | bytes 393224 | tf_op jit(solution)/shard_map/ppermute | solution.py:409
  10.1 3.2 %collective-permute-done.3 = f32[16,2048]{1,0:T(8,128)S(1)} collective-permute-done((f32[16,2048]{1,0:T(8,128)S(1)}, f32[16,2048]{1,0:T(8,128)S(1)}, u32[]{:S(2)}, u32[]{:S(2)}) %collective-permute-start.3) | collective-permute-done | bytes 131104 | tf_op jit(solution)/shard_map/ppermute | solution.py:410
  13.3 0.1 collective-permute-start.4
  13.4 0.0 collective-permute-done.1
  13.5 2.7 %collective-permute-start.2 = (f32[16,4096]{1,0:T(8,128)S(1)}, f32[16,4096]{1,0:T(8,128)S(1)}, u32[]{:S(2)}, u32[]{:S(2)}) collective-permute-start(f32[16,4096]{1,0:T(8,128)S(1)} %pad_add_fusion.1), channel_id=1, source_target_pairs={{0,2},{1,3},{2,4},{3,5},{4,6},{5,7},{6,0},{7,1},{8,10},{9,11},{10,... | collective-permute-start | bytes 786440 | tf_op jit(solution)/shard_map/ppermute | solution.py:414
  16.2 0.0 copy-done.3
  16.2 0.0 copy-done.2
  16.2 16.8 %geometry.1 = (f32[1024,1024]{1,0:T(8,128)S(1)}, f32[1024,1024]{1,0:T(8,128)S(1)}, f32[1024,1024]{1,0:T(8,128)S(1)}, f32[1024,1024]{1,0:T(8,128)S(1)}, f32[1024,1024]{1,0:T(8,128)S(1)}) custom-call(f32[3,2048]{1,0:T(4,128)S(1)} %copy-done.2, f32[3,1024]{1,0:T(4,128)S(1)} %copy-done.3), custom_call_target="tpu_custom_call" | custom-call | flops 83886080 | bytes 20971520 | tf_op jit(solution)/shard_map/geometry/pallas_call | solution.py:388
  33.0 0.0 collective-permute-done.4.down_ref
  33.1 0.0 collective-permute-done.2.up_ref
  33.1 30.6 %field.1 = f32[32,4,128]{2,1,0:T(4,128)S(1)} custom-call(f32[16,4096]{1,0:T(8,128)S(1)} %get-tuple-element.21.own_ref, f32[16,4096]{1,0:T(8,128)S(1)} %collective-permute-done.2.up_ref, f32[16,4096]{1,0:T(8,128)S(1)} %collective-permute-done.4.down_ref, f32[3,2048]{1,0:T(4,128)S(1)} %copy-done.2, bf16[128,1024]{1,0:T(8,128)(2,1)S(1)} %features.1.feature_ref, ...), custom_call_target="tpu_custom_call" | custom-call | tf_op jit(solution)/shard_map/field/pallas_call | solution.py:425
  63.7 19.7 %all_to_all.5.parts_ref = f32[32,4,128]{2,1,0:T(4,128)S(1)} all-to-all(f32[32,4,128]{2,1,0:T(4,128)S(1)} %field.1), channel_id=1, replica_groups=mesh['panel'=32,'obs'=8] {'panel'}, dimensions={0} | all-to-all | bytes 131072 | tf_op jit(solution)/shard_map/all_to_all | solution.py:441
  83.4 3.3 %collective-permute-start.5 = (f32[2,128]{1,0:T(2,128)S(1)}, f32[2,128]{1,0:T(2,128)S(1)}, u32[]{:S(2)}, u32[]{:S(2)}) collective-permute-start(f32[2,128]{1,0:T(2,128)S(1)} %get-tuple-element.32), channel_id=1, source_target_pairs={{0,1},{1,0},{2,3},{3,2},{4,5},{5,4},{6,7},{7,6},{8,9},{9,8},{10,11... | collective-permute-start | bytes 3080 | tf_op jit(solution)/shard_map/ppermute | solution.py:450
  86.7 0.8 collective-permute-done.5
  87.5 0.7 reshape.7
  (5 shorter events, 0.1 us)
Async XLA Ops:
  0.0 6.9 %copy-start = (bf16[8,64,192]{2,1,0:T(8,128)(2,1)S(1)}, bf16[8,64,192]{2,1,0:T(8,128)(2,1)}, u32[]{:S(2)}) copy-start(bf16[8,64,192]{2,1,0:T(8,128)(2,1)} %constant.4.clone.table_ref) | copy-start | bytes 589828
  0.0 16.2 %copy-start.3 = (f32[3,1024]{1,0:T(4,128)S(1)}, f32[3,1024]{1,0:T(4,128)}, u32[]{:S(2)}) copy-start(f32[3,1024]{1,0:T(4,128)} %obs_ref.1) | copy-start | bytes 36868
  0.0 16.2 %copy-start.2 = (f32[3,2048]{1,0:T(4,128)S(1)}, f32[3,2048]{1,0:T(4,128)}, u32[]{:S(2)}) copy-start(f32[3,2048]{1,0:T(4,128)} %pos_ref.3) | copy-start | bytes 73732
  2.2 0.8 copy-start.1
  2.9 0.7 copy-start.4
  4.6 2.3 %collective-permute-start = (f32[128,1024]{1,0:T(8,128)S(1)}, f32[128,1024]{1,0:T(8,128)S(1)}, u32[]{:S(2)}, u32[]{:S(2)}) collective-permute-start(f32[128,1024]{1,0:T(8,128)S(1)} %get-tuple-element.20), channel_id=1, source_target_pairs={{0,1},{1,0},{2,3},{3,2},{4,5},{5,4},{6,7},{7,6},{8,9},{9,8},{10,11... | collective-permute-start | bytes 1572872 | tf_op jit(solution)/shard_map/ppermute | solution.py:385
  7.3 6.0 %collective-permute-start.3 = (f32[16,2048]{1,0:T(8,128)S(1)}, f32[16,2048]{1,0:T(8,128)S(1)}, u32[]{:S(2)}, u32[]{:S(2)}) collective-permute-start(f32[16,2048]{1,0:T(8,128)S(1)} %get-tuple-element.25), channel_id=1, source_target_pairs={{0,6},{1,7},{2,0},{3,1},{4,2},{5,3},{6,4},{7,5},{8,14},{9,15},{10,... | collective-permute-start | bytes 393224 | tf_op jit(solution)/shard_map/ppermute | solution.py:410
  7.8 5.6 %collective-permute-start.1 = (f32[16,2048]{1,0:T(8,128)S(1)}, f32[16,2048]{1,0:T(8,128)S(1)}, u32[]{:S(2)}, u32[]{:S(2)}) collective-permute-start(f32[16,2048]{1,0:T(8,128)S(1)} %get-tuple-element.23), channel_id=1, source_target_pairs={{0,2},{1,3},{2,4},{3,5},{4,6},{5,7},{6,0},{7,1},{8,10},{9,11},{10,... | collective-permute-start | bytes 393224 | tf_op jit(solution)/shard_map/ppermute | solution.py:409
  13.3 19.7 %collective-permute-start.4 = (f32[16,4096]{1,0:T(8,128)S(1)}, f32[16,4096]{1,0:T(8,128)S(1)}, u32[]{:S(2)}, u32[]{:S(2)}) collective-permute-start(f32[16,4096]{1,0:T(8,128)S(1)} %pad_add_fusion), channel_id=1, source_target_pairs={{0,6},{1,7},{2,0},{3,1},{4,2},{5,3},{6,4},{7,5},{8,14},{9,15},{10,... | collective-permute-start | bytes 786440 | tf_op jit(solution)/shard_map/ppermute | solution.py:415
  13.5 19.6 %collective-permute-start.2 = (f32[16,4096]{1,0:T(8,128)S(1)}, f32[16,4096]{1,0:T(8,128)S(1)}, u32[]{:S(2)}, u32[]{:S(2)}) collective-permute-start(f32[16,4096]{1,0:T(8,128)S(1)} %pad_add_fusion.1), channel_id=1, source_target_pairs={{0,2},{1,3},{2,4},{3,5},{4,6},{5,7},{6,0},{7,1},{8,10},{9,11},{10,... | collective-permute-start | bytes 786440 | tf_op jit(solution)/shard_map/ppermute | solution.py:414
  83.4 4.1 %collective-permute-start.5 = (f32[2,128]{1,0:T(2,128)S(1)}, f32[2,128]{1,0:T(2,128)S(1)}, u32[]{:S(2)}, u32[]{:S(2)}) collective-permute-start(f32[2,128]{1,0:T(2,128)S(1)} %get-tuple-element.32), channel_id=1, source_target_pairs={{0,1},{1,0},{2,3},{3,2},{4,5},{5,4},{6,7},{7,6},{8,9},{9,8},{10,11... | collective-permute-start | bytes 3080 | tf_op jit(solution)/shard_map/ppermute | solution.py:450

commit v3 on v2

v3 whole, which is shorter than its diff:
```python
import functools
import math

import jax
import jax.numpy as jnp
import numpy as np
from jax import lax
from jax.experimental import pallas as pl
from jax.experimental.pallas import tpu as pltpu
from jax.sharding import PartitionSpec as P

TIME = 256
FREQ = 32
MACH_NUMBER = 0.3
SAMPLE_SPACING = 0.04
FOUR_PI = 4.0 * math.pi
BASE = 2.0 * math.pi / (TIME * SAMPLE_SPACING)

OBSERVERS = 1024
SLOTS = 2048
HALF = SLOTS // 2
STEPS = 32
CHIPS = 4
BAND = 8
LIST = 256
GROUP = 16
BATCH = 256
PIECES = 16
DEPTH = 128
MIB = 1 << 20

F32 = jnp.float32
BF16 = jnp.bfloat16


def sine_fits():
    node = np.cos((np.arange(400) + 0.5) * np.pi / 400) * 0.5 + 0.5
    square = node * 1.3**2
    angle = np.sqrt(square)
    table = []
    for values, degree in ((np.sin(angle) / angle, 5), (np.cos(angle), 6)):
        fit = np.polynomial.chebyshev.Chebyshev.fit(square, values, degree, domain=[0, 1.3**2])
        table.append([float(v) for v in fit.convert(kind=np.polynomial.Polynomial).coef])
    return table


SIN_FIT, COS_FIT = sine_fits()


def fourier_rows():
    place = lax.axis_index("obs")
    chip, core = lax.div(place, 2), lax.rem(place, 2)
    row = lax.broadcasted_iota(jnp.int32, (64, 64), 0)
    lane = lax.broadcasted_iota(jnp.int32, (64, 64), 1)
    band = (chip + row // 16) & 3
    harmonic = BAND * band + (row & 7) + 1
    step = 64 * chip + ((lane + 32 * core) & 63)
    turns = (harmonic * step + 64 * ((row // 8) & 1)) & (TIME - 1)
    return jnp.cos(turns.astype(F32) * (2.0 * math.pi / TIME)) * (2.0 / TIME)


def params(mib=16):
    return pltpu.CompilerParams(vmem_limit_bytes=mib * MIB)


def split(value):
    high = value.astype(BF16)
    low = (value - high.astype(F32)).astype(BF16)
    return high, low


def source_kernel(series_ref, pack_ref, keep_ref, send_ref):
    core = lax.rem(lax.axis_index("obs"), 2)
    area = pack_ref[3:6, :] * (pack_ref[9:10, :] >= 0).astype(F32)
    for pair in range(HALF // 128):
        blocks = []
        for side in range(2):
            lanes = slice(128 * (2 * pair + side), 128 * (2 * pair + side) + 128)
            field = [series_ref[f, :, lanes] for f in range(5)]
            b1, b2, b3 = area[0:1, lanes], area[1:2, lanes], area[2:3, lanes]
            bc = MACH_NUMBER * b1
            flux = b1 * field[1] + b2 * field[2] + b3 * field[3] + bc * field[0]
            blocks.append([flux] + [b * field[4] + bc * field[1 + i] for i, b in enumerate((b1, b2, b3))])
        lanes = slice(128 * pair, 128 * pair + 128)
        for f in range(4):
            even, odd = blocks[0][f], blocks[1][f]
            rows = slice(32 * f, 32 * f + 32)
            keep_ref[rows, lanes] = jnp.where(core == 0, even, odd)
            send_ref[rows, lanes] = jnp.where(core == 0, odd, even)


def feature_kernel(pack_ref, out_ref):
    x = pack_ref[6:9, 0:OBSERVERS]
    rows = jnp.concatenate(
        [
            jnp.ones((1, OBSERVERS), F32),
            x,
            x[0:1] * x[0:1] + x[1:2] * x[1:2] + x[2:3] * x[2:3],
        ],
        axis=0,
    )
    high = rows.astype(BF16).astype(F32)
    low = rows - high
    rest = jnp.zeros((1, OBSERVERS), F32)
    out_ref[...] = jnp.concatenate([high, high, low, rest] * BAND, axis=0).astype(BF16)


def band_kernel(keep_ref, recv_ref, own_ref, up_ref, down_ref, far_ref, mark_ref):
    mark_ref[...] = jnp.zeros(mark_ref.shape, F32)
    high, low = split(fourier_rows())
    table = jnp.concatenate([high, high, low], axis=1)
    for f in range(4):
        rows = slice(32 * f, 32 * f + 32)
        for tile in range(HALF // 256):
            lanes = slice(256 * tile, 256 * tile + 256)
            kh, kl = split(keep_ref[rows, lanes])
            rh, rl = split(recv_ref[rows, lanes])
            stack = jnp.concatenate([kh, rh, kl, rl, kh, rh], axis=0)
            part = jnp.dot(table, stack, preferred_element_type=F32)
            out = slice(HALF * f + 256 * tile, HALF * f + 256 * tile + 256)
            own_ref[:, out] = part[0:16]
            up_ref[:, out] = part[16:32]
            down_ref[:, out] = part[48:64]
            far_ref[:, out] = part[32:48]


def double(cosine, sine):
    twice = cosine + cosine
    return twice * cosine - 1.0, twice * sine


def geometry_kernel(pack_ref, mark_ref, geo_ref, wide_ref):
    place = lax.axis_index("obs")
    core = lax.rem(place, 2)
    chip = lax.div(place, 2)

    def tile_step(power, first, t):
        lanes = pl.ds(pl.multiple_of(t * 128, 128), 128)
        x = [jnp.broadcast_to(pack_ref[6 + i : 7 + i, lanes], (8, 128)) for i in range(3)]
        for g in range(16):
            rows = pl.ds(pl.multiple_of(first + 8 * g, 8), 8)
            square = None
            for i in range(3):
                delta = x[i] - wide_ref[i, 8 * g : 8 * g + 8, :]
                square = delta * delta if square is None else square + delta * delta
            inverse = lax.rsqrt(square)
            r = square * inverse
            half = r * (0.5 * BASE) - 0.5 * math.pi
            s2 = half * half
            sine = s2 * SIN_FIT[-1] + SIN_FIT[-2]
            for c in SIN_FIT[-3::-1]:
                sine = sine * s2 + c
            sine = sine * half
            cosine = s2 * COS_FIT[-1] + COS_FIT[-2]
            for c in COS_FIT[-3::-1]:
                cosine = cosine * s2 + c
            twice = sine + sine
            er = twice * sine - 1.0
            ei = twice * cosine
            amp = inverse * inverse * (inverse * (1.0 / FOUR_PI))
            if power == 0:
                gr, gi = amp, jnp.zeros_like(amp)
            else:
                cr, ci = er, ei
                for _ in range(3):
                    cr, ci = double(cr, ci)
                if power == 2:
                    cr, ci = double(cr, ci)
                elif power == 3:
                    dr, di = double(cr, ci)
                    cr, ci = cr * dr - ci * di, cr * di + ci * dr
                gr, gi = amp * cr, amp * ci
            geo_ref[0, rows, lanes] = r
            geo_ref[1, rows, lanes] = er
            geo_ref[2, rows, lanes] = ei
            geo_ref[3, rows, lanes] = gr
            geo_ref[4, rows, lanes] = gi

    def body(power):
        def chunk(c, carry):
            wide = pl.multiple_of(c * 256, 256)
            pos = jnp.where(
                core == 0, pack_ref[0:3, pl.ds(wide, 128)], pack_ref[0:3, pl.ds(wide + 128, 128)]
            )
            pos = jnp.concatenate([pos, jnp.zeros((5, 128), F32)], axis=0)
            y = jnp.transpose(pos)
            for i in range(3):
                wide_ref[i] = jnp.broadcast_to(y[:, i : i + 1], (128, 128))

            def tile(t, inner):
                tile_step(power, c * 128, t)
                return inner

            lax.fori_loop(0, OBSERVERS // 128, tile, 0)
            return carry

        lax.fori_loop(0, HALF // 128, chunk, 0)

    for power in range(CHIPS):
        pl.when(chip == power)(lambda power=power: body(power))


def build_left(spec, pack_ref, stage, left):
    core = lax.rem(lax.axis_index("obs"), 2)
    first_band = lax.div(lax.axis_index("obs"), 2) * BAND
    wave = (lax.broadcasted_iota(jnp.int32, (BAND, 128), 0) + (first_band + 1)).astype(F32) * BASE
    freq_of = lax.broadcasted_iota(jnp.int32, (128, 128), 1) // 16
    stage[...] = jnp.zeros(stage.shape, F32)

    def chunk(c, carry):
        wide = pl.multiple_of(c * 256, 256)
        y = jnp.where(
            core == 0, pack_ref[0:3, pl.ds(wide, 128)], pack_ref[0:3, pl.ds(wide + 128, 128)]
        )
        y = [y[i : i + 1] for i in range(3)]
        square = y[0] * y[0] + y[1] * y[1] + y[2] * y[2]
        flux = spec(0, c)
        load = [spec(1 + i, c) for i in range(3)]
        gains = (-wave * flux[1], wave * flux[0])
        moment = [
            -(y[0] * load[0][p] + y[1] * load[1][p] + y[2] * load[2][p]) for p in range(2)
        ]
        comps = []
        for p in range(2):
            g = gains[p]
            rows = [g * square + moment[p]]
            rows += [load[i][p] - 2.0 * (y[i] * g) for i in range(3)]
            comps.append(rows + [g])
        for p in range(2):
            comps.append([wave * moment[p]] + [wave * load[i][p] for i in range(3)])
        for comp, rows in enumerate(comps):
            for q, row in enumerate(rows):
                high = row.astype(BF16).astype(F32)
                for place, value in ((q, high), (5 + q, row - high), (10 + q, high)):
                    stage[pl.ds(128 * comp + place, 8, stride=16), :] = value
        for comp in range(4):
            turned = jnp.transpose(stage[128 * comp : 128 * comp + 128, :])
            for k in range(BAND):
                block = jnp.where(freq_of == k, turned, 0.0).astype(BF16)
                left[pl.ds(c * 8, 8), comp * BAND + k] = block.reshape(8, GROUP, DEPTH)
        return carry

    lax.fori_loop(0, HALF // 128, chunk, 0)


def field_kernel(
    own_ref, up_ref, down_ref, far_ref, pack_ref, feature_ref,
    geo_ref,
    out_ref, stage, left, ready, after, total,
):
    def spec(f, c):
        lanes = pl.ds(pl.multiple_of(HALF * f + c * 128, 128), 128)
        value = own_ref[:, lanes] + up_ref[:, lanes] + (down_ref[:, lanes] + far_ref[:, lanes])
        return value[0:8], value[8:16]

    build_left(spec, pack_ref, stage, left)
    total[...] = jnp.zeros(total.shape, F32)
    batches = HALF // BATCH
    steps = batches * (OBSERVERS // LIST)
    groups = BATCH // GROUP

    def product(target, i, part):
        t, b = lax.div(i, batches), lax.rem(i, batches)
        size = 32 * GROUP * groups // PIECES
        if PIECES <= groups:
            lhs = left[pl.ds(b * groups + part * (groups // PIECES), groups // PIECES)]
        else:
            cut = PIECES // groups
            span = 32 // cut
            lhs = left[b * groups + part // cut, span * (part % cut) : span * (part % cut) + span]
        rhs = feature_ref[:, pl.ds(pl.multiple_of(t * LIST, LIST), LIST)]
        target[part * size : part * size + size] = jnp.dot(
            lhs.reshape(size, DEPTH), rhs, preferred_element_type=F32
        )

    def consume(source, i, target, following):
        t, b = lax.div(i, batches), lax.rem(i, batches)
        for lane in range(LIST // 128):
            lanes = pl.ds(pl.multiple_of(t * LIST + 128 * lane, 128), 128)
            near = slice(128 * lane, 128 * lane + 128)
            acc = [total[t, lane * 16 + i] for i in range(16)]
            for sub in range(BATCH // 8):
                piece, rest = divmod((lane * (BATCH // 8) + sub) * PIECES, BATCH // 4)
                if rest == 0:
                    product(target, following, piece)
                rows = pl.ds(pl.multiple_of(b * BATCH + 8 * sub, 8), 8)
                r, er, ei, pr, pi = [geo_ref[i, rows, lanes] for i in range(5)]
                cr, ci = pr * er - pi * ei, pr * ei + pi * er
                twice = er + er
                for k in range(BAND):
                    m = []
                    for comp in range(4):
                        base = ((sub // 2) * 32 + comp * BAND + k) * GROUP + 8 * (sub % 2)
                        m.append(source[base : base + 8, near])
                    tr = m[0] - r * m[3]
                    ti = m[1] + r * m[2]
                    acc[2 * k] = acc[2 * k] + (cr * tr - ci * ti)
                    acc[2 * k + 1] = acc[2 * k + 1] + (cr * ti + ci * tr)
                    if k + 1 < BAND:
                        pr, pi, cr, ci = cr, ci, twice * cr - pr, twice * ci - pi
            for i in range(16):
                total[t, lane * 16 + i] = acc[i]

    for part in range(PIECES):
        product(ready, 0, part)

    def step(i, carry):
        following = jnp.minimum(i + 1, steps - 1)

        @pl.when(lax.rem(i, 2) == 0)
        def _():
            consume(ready, i, after, following)

        @pl.when(lax.rem(i, 2) == 1)
        def _():
            consume(after, i, ready, following)

        return carry

    lax.fori_loop(0, steps, step, 0)

    lane_block = lax.broadcasted_iota(jnp.int32, (4, 128), 1) // 32
    for t in range(OBSERVERS // LIST):
        for lane in range(LIST // 128):
            sums = [jnp.sum(total[t, lane * 16 + i], axis=0, keepdims=True) for i in range(16)]
            packs = [
                jnp.concatenate(
                    [sums[2 * kk], sums[2 * kk + 1], sums[2 * (4 + kk)], sums[2 * (4 + kk) + 1]],
                    axis=0,
                )
                for kk in range(4)
            ]
            for m in range(4):
                value = None
                for kk in range(4):
                    shift = (32 * (kk - m)) % 128
                    turned = pltpu.roll(packs[kk], shift, axis=1) if shift else packs[kk]
                    value = turned if value is None else jnp.where(lane_block == kk, turned, value)
                for h in range(2):
                    out_ref[2 * (8 * t + 4 * lane + m) + h] = value[2 * h : 2 * h + 2]


def finish_kernel(parts_ref, out_ref):
    value = jnp.sum(parts_ref[...], axis=0)
    for kk in range(4):
        out_ref[:, kk, :] = value[:, 32 * kk : 32 * kk + 32]


def shape(*dims, dtype=F32):
    return jax.ShapeDtypeStruct(dims, dtype)


def on_device(series, panel_pos, panel_area, observers, owner):
    whole = pl.BlockSpec(memory_space=pltpu.VMEM)
    pack = jnp.concatenate(
        [
            panel_pos,
            panel_area,
            jnp.pad(observers, ((0, 0), (0, SLOTS - OBSERVERS))),
            owner.astype(F32).reshape(1, SLOTS),
        ],
        axis=0,
    )
    keep, send = pl.pallas_call(
        source_kernel,
        out_shape=(shape(128, HALF), shape(128, HALF)),
        in_specs=[whole] * 2,
        out_specs=(whole,) * 2,
        compiler_params=params(),
        name="sources",
    )(jnp.transpose(series, (1, 0, 2)), pack)
    features = pl.pallas_call(
        feature_kernel,
        out_shape=shape(DEPTH, OBSERVERS, dtype=BF16),
        in_specs=[whole],
        out_specs=whole,
        compiler_params=params(),
        name="features",
    )(pack)
    swap = [(i, i ^ 1) for i in range(8)]
    above = [(i, (i + 2) % 8) for i in range(8)]
    below = [(i, (i + 6) % 8) for i in range(8)]
    recv = lax.ppermute(send, "obs", swap)

    pair_count = HALF * OBSERVERS
    own, up, down, far, mark = pl.pallas_call(
        band_kernel,
        out_shape=(shape(16, 4 * HALF),) * 4 + (shape(8, 128),),
        in_specs=[whole] * 2,
        out_specs=(whole,) * 5,
        compiler_params=params(),
        name="bands",
    )(keep, recv)

    geometry = pl.pallas_call(
        geometry_kernel,
        out_shape=shape(5, HALF, OBSERVERS),
        in_specs=[whole] * 2,
        out_specs=whole,
        scratch_shapes=[pltpu.VMEM((3, 128, 128), F32)],
        compiler_params=params(8),
        cost_estimate=pl.CostEstimate(
            flops=80 * pair_count, bytes_accessed=32 * MIB, transcendentals=0
        ),
        name="geometry",
    )(pack, mark)
    across = lax.ppermute(far, "obs", [(i, (i + 4) % 8) for i in range(8)])
    from_below = lax.ppermute(up, "obs", above)
    from_above = lax.ppermute(down, "obs", below)

    chunks = pl.pallas_call(
        field_kernel,
        out_shape=shape(64, 2, 128),
        in_specs=[whole] * 7,
        out_specs=whole,
        scratch_shapes=[
            pltpu.VMEM((512, 128), F32),
            pltpu.VMEM((HALF // GROUP, 32, GROUP, DEPTH), BF16),
            pltpu.VMEM((32 * BATCH, LIST), F32),
            pltpu.VMEM((32 * BATCH, LIST), F32),
            pltpu.VMEM((OBSERVERS // LIST, 32, 8, 128), F32),
        ],
        compiler_params=params(32),
        name="field",
    )(own, from_below, from_above, across, pack, features, geometry)

    members = [
        [8 * d + 2 * y + c for d in range(lax.axis_size("panel")) for c in range(2)]
        for y in range(CHIPS)
    ]
    parts = lax.all_to_all(
        chunks,
        ("panel", "obs"),
        split_axis=0,
        concat_axis=0,
        axis_index_groups=members,
        tiled=True,
    )
    value = pl.pallas_call(
        finish_kernel,
        out_shape=shape(2, 4, 32),
        in_specs=[whole],
        out_specs=whole,
        compiler_params=params(),
        name="finish",
    )(parts)
    return jnp.transpose(value, (2, 0, 1))


def solution(mesh):
    in_specs = (P("obs", None, "panel"), P(None, "panel"), P(None, "panel"), P(), P("panel"))
    out_specs = P("panel", None, "obs")
    return jax.shard_map(
        on_device, mesh=mesh, in_specs=in_specs, out_specs=out_specs, check_vma=False
    )
```

time: 88.4 us -> 74 us (0.84)
  starting transfers between devices: 9.59 us -> 3.79 us
  Pallas kernels: 48.8 us -> 43.8 us
  waiting for transfers between devices: 5.61 us -> 1.54 us
  local copies, waits for them, and re-layouts: 4.31 us -> 1.31 us
  blocking collectives: 19.7 us -> 21.8 us
  other arithmetic: 0.06 us -> 1.53 us
    pallas_call x5, Pallas kernels: 48.8 us -> 43.7 us  [the longest x1 28.3 us: on_device(): pl.pallas_call(field_kernel, out_shape=shape(64, 2, 128), in_specs=[whole...]
    ppermute x3 -> x1, starting transfers between devices: 6.02 us -> 1.27 us  [on_device(): across = lax.ppermute(far, 'obs', [(i, (i + 4) % 8) for i in range(8)])]
    ppermute x3 -> x1, waiting for transfers between devices: 4.07 us -> 0.01 us  [on_device(): across = lax.ppermute(far, 'obs', [(i, (i + 4) % 8) for i in range(8)])]
    unnamed x11 -> x2, local copies, waits for them, and re-layouts: 3.63 us -> 1.31 us
    all_to_all x1, blocking collectives: 19.7 us -> 21.8 us  [on_device(): lax.all_to_all(chunks, ('panel', 'obs'), split_axis=0, concat_axis=0, axi...]
    ppermute x1, starting transfers between devices: 2.73 us -> 1.75 us  [on_device(): from_below = lax.ppermute(up, 'obs', above)]
  transfers between devices with their start and end apart: 6 -> 4, of which waited for: 3 -> 1; matrix products, arithmetic and copies ran while one was open for 0% -> 0% of each run, Pallas kernels for 19% -> 19%
where the time goes in v3:
time: 74 us; the launch traced here: 73.8 us
  Pallas kernels  43.8 us (59%)
  blocking collectives  21.8 us (29%)
  starting transfers between devices  3.79 us (5%)
  waiting for transfers between devices  1.54 us (2%)
  other arithmetic  1.53 us (2%)
  local copies, waits for them, and re-layouts  1.31 us (2%)
    pallas_call x1, Pallas kernels, on_device(): pl.pallas_call(field_kernel, out_shape=shape(64, 2, 128), in_specs=[whole...  28.3 us
    all_to_all x1, blocking collectives, on_device(): lax.all_to_all(chunks, ('panel', 'obs'), split_axis=0, concat_axis=0, axi...  21.8 us
    pallas_call x1, Pallas kernels, on_device(): pl.pallas_call(geometry_kernel, out_shape=shape(5, HALF, OBSERVERS), in_s...  14 us
    ppermute x1, starting transfers between devices, on_device(): from_below = lax.ppermute(up, 'obs', above)  1.75 us
    ppermute x1, waiting for transfers between devices, on_device(): recv = lax.ppermute(send, 'obs', swap)  1.54 us
  transfers between devices with their start and end apart: 4, of which 1 were waited for; matrix products, arithmetic and copies ran while one was open for 0% of the time, Pallas kernels for 19%

profile of v3, /device:TPU:25, one launch (start us, length us, event | category | flops | bytes accessed | tf_op | source)
XLA Modules:
  0.0 73.8 jit_solution(12765596405831420666)
XLA Ops:
  0.0 0.7 convert_element_type.5
  0.7 0.8 %fusion.pack_ref = f32[10,2048]{1,0:T(8,128)S(1)} fusion(f32[3,1024]{1,0:T(4,128)} %param.8, f32[1,2048]{1,0:T(1,128)S(1)} %bitcast.4, f32[3,2048]{1,0:T(4,128)} %param.7, f32[3,2048]{1,0:T(4,128)} %param.6), kind=kLoop, calls=%fused_computation.3 | loop fusion | flops 143360 | bytes 151552 | tf_op jit(solution)/shard_map/concatenate | solution.py:355
  1.5 0.0 copy-start
  1.5 1.3 %copy-done = f32[32,5,2048]{2,0,1:T(8,128)S(1)} copy-done((f32[32,5,2048]{2,0,1:T(8,128)S(1)}, f32[32,5,2048]{2,0,1:T(8,128)}, u32[]{:S(2)}) %copy-start) | copy-done | bytes 1310744
  2.9 0.2 sources.1
  3.1 0.8 %collective-permute-start = (f32[128,1024]{1,0:T(8,128)S(1)}, f32[128,1024]{1,0:T(8,128)S(1)}, u32[]{:S(2)}, u32[]{:S(2)}) collective-permute-start(f32[128,1024]{1,0:T(8,128)S(1)} %get-tuple-element.13), channel_id=1, source_target_pairs={{0,1},{1,0},{2,3},{3,2},{4,5},{5,4},{6,7},{7,6},{8,9},{9,8},{10,11... | collective-permute-start | bytes 1572872 | tf_op jit(solution)/shard_map/ppermute | solution.py:383
  3.8 1.5 %collective-permute-done.recv_ref = f32[128,1024]{1,0:T(8,128)S(1)} collective-permute-done((f32[128,1024]{1,0:T(8,128)S(1)}, f32[128,1024]{1,0:T(8,128)S(1)}, u32[]{:S(2)}, u32[]{:S(2)}) %collective-permute-start) | collective-permute-done | bytes 524320 | tf_op jit(solution)/shard_map/ppermute | solution.py:383
  5.4 0.6 bands.1
  5.9 1.8 %collective-permute-start.1 = (f32[16,4096]{1,0:T(8,128)S(1)}, f32[16,4096]{1,0:T(8,128)S(1)}, u32[]{:S(2)}, u32[]{:S(2)}) collective-permute-start(f32[16,4096]{1,0:T(8,128)S(1)} %get-tuple-element.15), channel_id=1, source_target_pairs={{0,2},{1,3},{2,4},{3,5},{4,6},{5,7},{6,0},{7,1},{8,10},{9,11},{10,... | collective-permute-start | bytes 786440 | tf_op jit(solution)/shard_map/ppermute | solution.py:408
  7.7 0.0 collective-permute-start.2
  7.7 1.3 %collective-permute-start.3 = (f32[16,4096]{1,0:T(8,128)S(1)}, f32[16,4096]{1,0:T(8,128)S(1)}, u32[]{:S(2)}, u32[]{:S(2)}) collective-permute-start(f32[16,4096]{1,0:T(8,128)S(1)} %get-tuple-element.17), channel_id=1, source_target_pairs={{0,4},{1,5},{2,6},{3,7},{4,0},{5,1},{6,2},{7,3},{8,12},{9,13},{10,... | collective-permute-start | bytes 786440 | tf_op jit(solution)/shard_map/ppermute | solution.py:407
  9.0 14.0 %geometry.1.geo_ref = f32[5,1024,1024]{2,1,0:T(8,128)S(1)} custom-call(f32[10,2048]{1,0:T(8,128)S(1)} %fusion.pack_ref, f32[8,128]{1,0:T(8,128)S(1)} %get-tuple-element.18.mark_ref), custom_call_target="tpu_custom_call" | custom-call | flops 83886080 | bytes 33554432 | tf_op jit(solution)/shard_map/geometry/pallas_call | solution.py:395
  23.0 0.0 collective-permute-done.1.up_ref
  23.0 0.0 collective-permute-done.2.down_ref
  23.0 0.0 collective-permute-done.3.far_ref
  23.0 28.3 %field.1 = f32[64,2,128]{2,1,0:T(2,128)S(1)} custom-call(f32[16,4096]{1,0:T(8,128)S(1)} %get-tuple-element.14.own_ref, f32[16,4096]{1,0:T(8,128)S(1)} %collective-permute-done.1.up_ref, f32[16,4096]{1,0:T(8,128)S(1)} %collective-permute-done.2.down_ref, f32[16,4096]{1,0:T(8,128)S(1)} %collective-permute-done.3.far_ref, f32[10,2048]{1,0:T(8,128)S(1)} %fusion.pack_ref, ...), custom_call_target="tpu_custom_call" | custom-call | tf_op jit(solution)/shard_map/field/pallas_call | solution.py:411
  51.3 21.8 %all_to_all.5.parts_ref = f32[64,2,128]{2,1,0:T(2,128)S(1)} all-to-all(f32[64,2,128]{2,1,0:T(2,128)S(1)} %field.1), channel_id=1, replica_groups={{0,1,8,9,16,17,24,25,32,33,40,41,48,49,56,57,64,65,72,73,80,81,88,89,96..., dimensions={0} | all-to-all | bytes 131072 | tf_op jit(solution)/shard_map/all_to_all | solution.py:431
  73.0 0.7 finish.1
  (1 shorter events, 0.0 us)
Async XLA Ops:
  1.5 1.3 %copy-start = (f32[32,5,2048]{2,0,1:T(8,128)S(1)}, f32[32,5,2048]{2,0,1:T(8,128)}, u32[]{:S(2)}) copy-start(f32[32,5,2048]{2,0,1:T(8,128)} %param.5) | copy-start | bytes 3932164
  3.1 2.3 %collective-permute-start = (f32[128,1024]{1,0:T(8,128)S(1)}, f32[128,1024]{1,0:T(8,128)S(1)}, u32[]{:S(2)}, u32[]{:S(2)}) collective-permute-start(f32[128,1024]{1,0:T(8,128)S(1)} %get-tuple-element.13), channel_id=1, source_target_pairs={{0,1},{1,0},{2,3},{3,2},{4,5},{5,4},{6,7},{7,6},{8,9},{9,8},{10,11... | collective-permute-start | bytes 1572872 | tf_op jit(solution)/shard_map/ppermute | solution.py:383
  5.9 17.0 %collective-permute-start.1 = (f32[16,4096]{1,0:T(8,128)S(1)}, f32[16,4096]{1,0:T(8,128)S(1)}, u32[]{:S(2)}, u32[]{:S(2)}) collective-permute-start(f32[16,4096]{1,0:T(8,128)S(1)} %get-tuple-element.15), channel_id=1, source_target_pairs={{0,2},{1,3},{2,4},{3,5},{4,6},{5,7},{6,0},{7,1},{8,10},{9,11},{10,... | collective-permute-start | bytes 786440 | tf_op jit(solution)/shard_map/ppermute | solution.py:408
  7.7 15.3 %collective-permute-start.2 = (f32[16,4096]{1,0:T(8,128)S(1)}, f32[16,4096]{1,0:T(8,128)S(1)}, u32[]{:S(2)}, u32[]{:S(2)}) collective-permute-start(f32[16,4096]{1,0:T(8,128)S(1)} %get-tuple-element.16), channel_id=1, source_target_pairs={{0,6},{1,7},{2,0},{3,1},{4,2},{5,3},{6,4},{7,5},{8,14},{9,15},{10,... | collective-permute-start | bytes 786440 | tf_op jit(solution)/shard_map/ppermute | solution.py:409
  7.7 15.3 %collective-permute-start.3 = (f32[16,4096]{1,0:T(8,128)S(1)}, f32[16,4096]{1,0:T(8,128)S(1)}, u32[]{:S(2)}, u32[]{:S(2)}) collective-permute-start(f32[16,4096]{1,0:T(8,128)S(1)} %get-tuple-element.17), channel_id=1, source_target_pairs={{0,4},{1,5},{2,6},{3,7},{4,0},{5,1},{6,2},{7,3},{8,12},{9,13},{10,... | collective-permute-start | bytes 786440 | tf_op jit(solution)/shard_map/ppermute | solution.py:407

commit v4 on v3

--- a/solution.py
+++ b/solution.py
@@ -26,6 +26,7 @@
 GROUP = 16
 BATCH = 256
 PIECES = 16
+EARLY = 1
 DEPTH = 128
 MIB = 1 << 20
 
@@ -35,11 +36,11 @@
 
 def sine_fits():
     node = np.cos((np.arange(400) + 0.5) * np.pi / 400) * 0.5 + 0.5
-    square = node * 1.3**2
+    square = node * 0.66**2
     angle = np.sqrt(square)
     table = []
-    for values, degree in ((np.sin(angle) / angle, 5), (np.cos(angle), 6)):
-        fit = np.polynomial.chebyshev.Chebyshev.fit(square, values, degree, domain=[0, 1.3**2])
+    for values, degree in ((np.sin(angle) / angle, 3), (np.cos(angle), 4)):
+        fit = np.polynomial.chebyshev.Chebyshev.fit(square, values, degree, domain=[0, 0.66**2])
         table.append([float(v) for v in fit.convert(kind=np.polynomial.Polynomial).coef])
     return table
 
@@ -69,7 +70,8 @@
     return high, low
 
 
-def source_kernel(series_ref, pack_ref, keep_ref, send_ref):
+def source_kernel(series_ref, pack_ref, keep_ref, send_ref, mark_ref):
+    mark_ref[...] = jnp.zeros(mark_ref.shape, F32)
     core = lax.rem(lax.axis_index("obs"), 2)
     area = pack_ref[3:6, :] * (pack_ref[9:10, :] >= 0).astype(F32)
     for pair in range(HALF // 128):
@@ -105,8 +107,8 @@
     out_ref[...] = jnp.concatenate([high, high, low, rest] * BAND, axis=0).astype(BF16)
 
 
-def band_kernel(keep_ref, recv_ref, own_ref, up_ref, down_ref, far_ref, mark_ref):
-    mark_ref[...] = jnp.zeros(mark_ref.shape, F32)
+def band_kernel(keep_ref, recv_ref, given_ref, own_ref, up_ref, down_ref, far_ref, mark_ref):
+    mark_ref[...] = given_ref[...]
     high, low = split(fourier_rows())
     table = jnp.concatenate([high, high, low], axis=1)
     for f in range(4):
@@ -129,7 +131,18 @@
     return twice * cosine - 1.0, twice * sine
 
 
-def geometry_kernel(pack_ref, mark_ref, geo_ref, wide_ref):
+def early_kernel(pack_ref, mark_ref, geo_ref, done_ref, wide_ref):
+    done_ref[...] = mark_ref[...]
+    geometry_chunks(0, EARLY, pack_ref, geo_ref, wide_ref)
+
+
+def geometry_kernel(pack_ref, mark_ref, early_ref, geo_ref, wide_ref):
+    for i in range(6):
+        geo_ref[i, 0 : 128 * EARLY, :] = early_ref[i]
+    geometry_chunks(EARLY, HALF // 128, pack_ref, geo_ref, wide_ref)
+
+
+def geometry_chunks(first_chunk, last_chunk, pack_ref, geo_ref, wide_ref):
     place = lax.axis_index("obs")
     core = lax.rem(place, 2)
     chip = lax.div(place, 2)
@@ -145,15 +158,16 @@
                 square = delta * delta if square is None else square + delta * delta
             inverse = lax.rsqrt(square)
             r = square * inverse
-            half = r * (0.5 * BASE) - 0.5 * math.pi
-            s2 = half * half
+            quarter = r * (0.25 * BASE) - 0.25 * math.pi
+            s2 = quarter * quarter
             sine = s2 * SIN_FIT[-1] + SIN_FIT[-2]
             for c in SIN_FIT[-3::-1]:
                 sine = sine * s2 + c
-            sine = sine * half
+            sine = sine * quarter
             cosine = s2 * COS_FIT[-1] + COS_FIT[-2]
             for c in COS_FIT[-3::-1]:
                 cosine = cosine * s2 + c
+            cosine, sine = double(cosine, sine)
             twice = sine + sine
             er = twice * sine - 1.0
             ei = twice * cosine
@@ -170,11 +184,9 @@
                     dr, di = double(cr, ci)
                     cr, ci = cr * dr - ci * di, cr * di + ci * dr
                 gr, gi = amp * cr, amp * ci
-            geo_ref[0, rows, lanes] = r
-            geo_ref[1, rows, lanes] = er
-            geo_ref[2, rows, lanes] = ei
-            geo_ref[3, rows, lanes] = gr
-            geo_ref[4, rows, lanes] = gi
+            br, bi = (gr * er, gr * ei) if power == 0 else (gr * er - gi * ei, gr * ei + gi * er)
+            for i, value in enumerate((r, er + er, gr, gi, br, bi)):
+                geo_ref[i, rows, lanes] = value
 
     def body(power):
         def chunk(c, carry):
@@ -194,7 +206,7 @@
             lax.fori_loop(0, OBSERVERS // 128, tile, 0)
             return carry
 
-        lax.fori_loop(0, HALF // 128, chunk, 0)
+        lax.fori_loop(first_chunk, last_chunk, chunk, 0)
 
     for power in range(CHIPS):
         pl.when(chip == power)(lambda power=power: body(power))
@@ -275,18 +287,17 @@
 
     def consume(source, i, target, following):
         t, b = lax.div(i, batches), lax.rem(i, batches)
+        sums = []
         for lane in range(LIST // 128):
             lanes = pl.ds(pl.multiple_of(t * LIST + 128 * lane, 128), 128)
             near = slice(128 * lane, 128 * lane + 128)
-            acc = [total[t, lane * 16 + i] for i in range(16)]
+            acc = [None] * 16
             for sub in range(BATCH // 8):
                 piece, rest = divmod((lane * (BATCH // 8) + sub) * PIECES, BATCH // 4)
                 if rest == 0:
                     product(target, following, piece)
                 rows = pl.ds(pl.multiple_of(b * BATCH + 8 * sub, 8), 8)
-                r, er, ei, pr, pi = [geo_ref[i, rows, lanes] for i in range(5)]
-                cr, ci = pr * er - pi * ei, pr * ei + pi * er
-                twice = er + er
+                r, twice, pr, pi, cr, ci = [geo_ref[i, rows, lanes] for i in range(6)]
                 for k in range(BAND):
                     m = []
                     for comp in range(4):
@@ -294,12 +305,13 @@
                         m.append(source[base : base + 8, near])
                     tr = m[0] - r * m[3]
                     ti = m[1] + r * m[2]
-                    acc[2 * k] = acc[2 * k] + (cr * tr - ci * ti)
-                    acc[2 * k + 1] = acc[2 * k + 1] + (cr * ti + ci * tr)
+                    for slot, term in ((2 * k, cr * tr - ci * ti), (2 * k + 1, cr * ti + ci * tr)):
+                        acc[slot] = term if acc[slot] is None else acc[slot] + term
                     if k + 1 < BAND:
                         pr, pi, cr, ci = cr, ci, twice * cr - pr, twice * ci - pi
-            for i in range(16):
-                total[t, lane * 16 + i] = acc[i]
+            sums += acc
+        for i in range(32):
+            total[t, i] = total[t, i] + sums[i]
 
     for part in range(PIECES):
         product(ready, 0, part)
@@ -361,11 +373,11 @@
         ],
         axis=0,
     )
-    keep, send = pl.pallas_call(
+    keep, send, begun = pl.pallas_call(
         source_kernel,
-        out_shape=(shape(128, HALF), shape(128, HALF)),
+        out_shape=(shape(128, HALF), shape(128, HALF), shape(8, 128)),
         in_specs=[whole] * 2,
-        out_specs=(whole,) * 2,
+        out_specs=(whole,) * 3,
         compiler_params=params(),
         name="sources",
     )(jnp.transpose(series, (1, 0, 2)), pack)
@@ -383,19 +395,31 @@
     recv = lax.ppermute(send, "obs", swap)
 
     pair_count = HALF * OBSERVERS
+    early, ready = pl.pallas_call(
+        early_kernel,
+        out_shape=(shape(6, 128 * EARLY, OBSERVERS), shape(8, 128)),
+        in_specs=[whole] * 2,
+        out_specs=(whole, whole),
+        scratch_shapes=[pltpu.VMEM((3, 128, 128), F32)],
+        compiler_params=params(8),
+        cost_estimate=pl.CostEstimate(
+            flops=10 * pair_count, bytes_accessed=4 * MIB, transcendentals=0
+        ),
+        name="early",
+    )(pack, begun)
     own, up, down, far, mark = pl.pallas_call(
         band_kernel,
         out_shape=(shape(16, 4 * HALF),) * 4 + (shape(8, 128),),
-        in_specs=[whole] * 2,
+        in_specs=[whole] * 3,
         out_specs=(whole,) * 5,
         compiler_params=params(),
         name="bands",
-    )(keep, recv)
+    )(keep, recv, ready)
 
     geometry = pl.pallas_call(
         geometry_kernel,
-        out_shape=shape(5, HALF, OBSERVERS),
-        in_specs=[whole] * 2,
+        out_shape=shape(6, HALF, OBSERVERS),
+        in_specs=[whole] * 3,
         out_specs=whole,
         scratch_shapes=[pltpu.VMEM((3, 128, 128), F32)],
         compiler_params=params(8),
@@ -403,7 +427,7 @@
             flops=80 * pair_count, bytes_accessed=32 * MIB, transcendentals=0
         ),
         name="geometry",
-    )(pack, mark)
+    )(pack, mark, early)
     across = lax.ppermute(far, "obs", [(i, (i + 4) % 8) for i in range(8)])
     from_below = lax.ppermute(up, "obs", above)
     from_above = lax.ppermute(down, "obs", below)
@@ -420,7 +444,7 @@
             pltpu.VMEM((32 * BATCH, LIST), F32),
             pltpu.VMEM((OBSERVERS // LIST, 32, 8, 128), F32),
         ],
-        compiler_params=params(32),
+        compiler_params=params(28),
         name="field",
     )(own, from_below, from_above, across, pack, features, geometry)
 

time: 74 us -> 72.2 us (0.976)
  waiting for transfers between devices: 1.54 us -> 0.01 us
  Pallas kernels: 43.8 us -> 42.9 us
    pallas_call x1, Pallas kernels: 28.3 us -> 26.5 us  [on_device(): pl.pallas_call(field_kernel, out_shape=shape(64, 2, 128), in_specs=[whole...]
    ppermute x1, waiting for transfers between devices: 1.54 us -> 0.01 us  [on_device(): recv = lax.ppermute(send, 'obs', swap)]
    pallas_call x1 -> x2, Pallas kernels: 14 us -> 14.9 us  [the longest x1 13.3 us: on_device(): pl.pallas_call(geometry_kernel, out_shape=shape(6, HALF, OBSERVERS), in_s...]
  transfers between devices with their start and end apart: 4 -> 4, of which waited for: 1 -> 0; matrix products, arithmetic and copies ran while one was open for 0% -> 0% of each run, Pallas kernels for 19% -> 21%
where the time goes in v4:
time: 72.2 us; the launch traced here: 71.3 us
  Pallas kernels  42.9 us (59%)
  blocking collectives  21.8 us (30%)
  starting transfers between devices  3.72 us (5%)
  other arithmetic  1.53 us (2%)
  local copies, waits for them, and re-layouts  1.31 us (2%)
    pallas_call x1, Pallas kernels, on_device(): pl.pallas_call(field_kernel, out_shape=shape(64, 2, 128), in_specs=[whole...  26.5 us
    all_to_all x1, blocking collectives, on_device(): lax.all_to_all(chunks, ('panel', 'obs'), split_axis=0, concat_axis=0, axi...  21.8 us
    pallas_call x1, Pallas kernels, on_device(): pl.pallas_call(geometry_kernel, out_shape=shape(6, HALF, OBSERVERS), in_s...  13.3 us
    ppermute x1, starting transfers between devices, on_device(): from_below = lax.ppermute(up, 'obs', above)  1.68 us
    pallas_call x1, Pallas kernels, on_device(): pl.pallas_call(early_kernel, out_shape=(shape(6, 128 * EARLY, OBSERVERS),...  1.59 us
  transfers between devices with their start and end apart: 4, of which 0 were waited for; matrix products, arithmetic and copies ran while one was open for 0% of the time, Pallas kernels for 21%

profile of v4, /device:TPU:25, one launch (start us, length us, event | category | flops | bytes accessed | tf_op | source)
XLA Modules:
  0.0 71.3 jit_solution(3722710679535131018)
XLA Ops:
  0.0 0.7 convert_element_type.5
  0.7 0.8 %fusion.pack_ref = f32[10,2048]{1,0:T(8,128)S(1)} fusion(f32[3,1024]{1,0:T(4,128)} %param.8, f32[1,2048]{1,0:T(1,128)S(1)} %bitcast.4, f32[3,2048]{1,0:T(4,128)} %param.7, f32[3,2048]{1,0:T(4,128)} %param.6), kind=kLoop, calls=%fused_computation.3 | loop fusion | flops 143360 | bytes 151552 | tf_op jit(solution)/shard_map/concatenate | solution.py:367
  1.5 0.0 copy-start
  1.5 1.3 %copy-done = f32[32,5,2048]{2,0,1:T(8,128)S(1)} copy-done((f32[32,5,2048]{2,0,1:T(8,128)S(1)}, f32[32,5,2048]{2,0,1:T(8,128)}, u32[]{:S(2)}) %copy-start) | copy-done | bytes 1310744
  2.9 0.2 sources.1
  3.1 0.8 %collective-permute-start = (f32[128,1024]{1,0:T(8,128)S(1)}, f32[128,1024]{1,0:T(8,128)S(1)}, u32[]{:S(2)}, u32[]{:S(2)}) collective-permute-start(f32[128,1024]{1,0:T(8,128)S(1)} %get-tuple-element.16), channel_id=1, source_target_pairs={{0,1},{1,0},{2,3},{3,2},{4,5},{5,4},{6,7},{7,6},{8,9},{9,8},{10,11... | collective-permute-start | bytes 1572872 | tf_op jit(solution)/shard_map/ppermute | solution.py:395
  3.8 1.6 %early.1 = (f32[6,128,1024]{2,1,0:T(8,128)S(1)}, f32[8,128]{1,0:T(8,128)S(1)}) custom-call(f32[10,2048]{1,0:T(8,128)S(1)} %fusion.pack_ref, f32[8,128]{1,0:T(8,128)S(1)} %get-tuple-element.17.mark_ref), custom_call_target="tpu_custom_call" | custom-call | flops 10485760 | bytes 4194304 | tf_op jit(solution)/shard_map/early/pallas_call | solution.py:398
  5.4 0.0 collective-permute-done.recv_ref
  5.4 0.6 bands.1
  6.0 1.7 %collective-permute-start.1 = (f32[16,4096]{1,0:T(8,128)S(1)}, f32[16,4096]{1,0:T(8,128)S(1)}, u32[]{:S(2)}, u32[]{:S(2)}) collective-permute-start(f32[16,4096]{1,0:T(8,128)S(1)} %get-tuple-element.20), channel_id=1, source_target_pairs={{0,2},{1,3},{2,4},{3,5},{4,6},{5,7},{6,0},{7,1},{8,10},{9,11},{10,... | collective-permute-start | bytes 786440 | tf_op jit(solution)/shard_map/ppermute | solution.py:432
  7.7 0.0 collective-permute-start.2
  7.7 1.3 %collective-permute-start.3 = (f32[16,4096]{1,0:T(8,128)S(1)}, f32[16,4096]{1,0:T(8,128)S(1)}, u32[]{:S(2)}, u32[]{:S(2)}) collective-permute-start(f32[16,4096]{1,0:T(8,128)S(1)} %get-tuple-element.22), channel_id=1, source_target_pairs={{0,4},{1,5},{2,6},{3,7},{4,0},{5,1},{6,2},{7,3},{8,12},{9,13},{10,... | collective-permute-start | bytes 786440 | tf_op jit(solution)/shard_map/ppermute | solution.py:431
  9.0 13.3 %geometry.1.geo_ref = f32[6,1024,1024]{2,1,0:T(8,128)S(1)} custom-call(f32[10,2048]{1,0:T(8,128)S(1)} %fusion.pack_ref, f32[8,128]{1,0:T(8,128)S(1)} %get-tuple-element.23.mark_ref, f32[6,128,1024]{2,1,0:T(8,128)S(1)} %get-tuple-element.24.early_ref), custom_call_target="tpu_custom_call" | custom-call | flops 83886080 | bytes 33554432 | tf_op jit(solution)/shard_map/geometry/pallas_call | solution.py:419
  22.3 0.0 collective-permute-done.1.up_ref
  22.3 0.0 collective-permute-done.2.down_ref
  22.3 0.0 collective-permute-done.3.far_ref
  22.3 26.5 %field.1 = f32[64,2,128]{2,1,0:T(2,128)S(1)} custom-call(f32[16,4096]{1,0:T(8,128)S(1)} %get-tuple-element.19.own_ref, f32[16,4096]{1,0:T(8,128)S(1)} %collective-permute-done.1.up_ref, f32[16,4096]{1,0:T(8,128)S(1)} %collective-permute-done.2.down_ref, f32[16,4096]{1,0:T(8,128)S(1)} %collective-permute-done.3.far_ref, f32[10,2048]{1,0:T(8,128)S(1)} %fusion.pack_ref, ...), custom_call_target="tpu_custom_call" | custom-call | tf_op jit(solution)/shard_map/field/pallas_call | solution.py:435
  48.8 21.8 %all_to_all.5.parts_ref = f32[64,2,128]{2,1,0:T(2,128)S(1)} all-to-all(f32[64,2,128]{2,1,0:T(2,128)S(1)} %field.1), channel_id=1, replica_groups={{0,1,8,9,16,17,24,25,32,33,40,41,48,49,56,57,64,65,72,73,80,81,88,89,96..., dimensions={0} | all-to-all | bytes 131072 | tf_op jit(solution)/shard_map/all_to_all | solution.py:455
  70.6 0.7 %finish.1 = f32[2,4,32]{2,1,0:T(4,128)} custom-call(f32[64,2,128]{2,1,0:T(2,128)S(1)} %all_to_all.5.parts_ref), custom_call_target="tpu_custom_call" | custom-call | tf_op jit(solution)/shard_map/finish/pallas_call | solution.py:463
  (1 shorter events, 0.0 us)
Async XLA Ops:
  1.5 1.3 %copy-start = (f32[32,5,2048]{2,0,1:T(8,128)S(1)}, f32[32,5,2048]{2,0,1:T(8,128)}, u32[]{:S(2)}) copy-start(f32[32,5,2048]{2,0,1:T(8,128)} %param.5) | copy-start | bytes 3932164
  3.1 2.4 %collective-permute-start = (f32[128,1024]{1,0:T(8,128)S(1)}, f32[128,1024]{1,0:T(8,128)S(1)}, u32[]{:S(2)}, u32[]{:S(2)}) collective-permute-start(f32[128,1024]{1,0:T(8,128)S(1)} %get-tuple-element.16), channel_id=1, source_target_pairs={{0,1},{1,0},{2,3},{3,2},{4,5},{5,4},{6,7},{7,6},{8,9},{9,8},{10,11... | collective-permute-start | bytes 1572872 | tf_op jit(solution)/shard_map/ppermute | solution.py:395
  6.0 16.3 %collective-permute-start.1 = (f32[16,4096]{1,0:T(8,128)S(1)}, f32[16,4096]{1,0:T(8,128)S(1)}, u32[]{:S(2)}, u32[]{:S(2)}) collective-permute-start(f32[16,4096]{1,0:T(8,128)S(1)} %get-tuple-element.20), channel_id=1, source_target_pairs={{0,2},{1,3},{2,4},{3,5},{4,6},{5,7},{6,0},{7,1},{8,10},{9,11},{10,... | collective-permute-start | bytes 786440 | tf_op jit(solution)/shard_map/ppermute | solution.py:432
  7.7 14.6 %collective-permute-start.2 = (f32[16,4096]{1,0:T(8,128)S(1)}, f32[16,4096]{1,0:T(8,128)S(1)}, u32[]{:S(2)}, u32[]{:S(2)}) collective-permute-start(f32[16,4096]{1,0:T(8,128)S(1)} %get-tuple-element.21), channel_id=1, source_target_pairs={{0,6},{1,7},{2,0},{3,1},{4,2},{5,3},{6,4},{7,5},{8,14},{9,15},{10,... | collective-permute-start | bytes 786440 | tf_op jit(solution)/shard_map/ppermute | solution.py:433
  7.7 14.6 %collective-permute-start.3 = (f32[16,4096]{1,0:T(8,128)S(1)}, f32[16,4096]{1,0:T(8,128)S(1)}, u32[]{:S(2)}, u32[]{:S(2)}) collective-permute-start(f32[16,4096]{1,0:T(8,128)S(1)} %get-tuple-element.22), channel_id=1, source_target_pairs={{0,4},{1,5},{2,6},{3,7},{4,0},{5,1},{6,2},{7,3},{8,12},{9,13},{10,... | collective-permute-start | bytes 786440 | tf_op jit(solution)/shard_map/ppermute | solution.py:431

commit v5 on v4

--- a/solution.py
+++ b/solution.py
@@ -252,7 +252,7 @@
                 left[pl.ds(c * 8, 8), comp * BAND + k] = block.reshape(8, GROUP, DEPTH)
         return carry
 
-    lax.fori_loop(0, HALF // 128, chunk, 0)
+    return chunk
 
 
 def field_kernel(
@@ -265,7 +265,7 @@
         value = own_ref[:, lanes] + up_ref[:, lanes] + (down_ref[:, lanes] + far_ref[:, lanes])
         return value[0:8], value[8:16]
 
-    build_left(spec, pack_ref, stage, left)
+    chunk = build_left(spec, pack_ref, stage, left)
     total[...] = jnp.zeros(total.shape, F32)
     batches = HALF // BATCH
     steps = batches * (OBSERVERS // LIST)
@@ -313,8 +313,13 @@
         for i in range(32):
             total[t, i] = total[t, i] + sums[i]
 
-    for part in range(PIECES):
-        product(ready, 0, part)
+    ahead = BATCH // 128
+    later = HALF // 128 - ahead
+    lax.fori_loop(0, ahead, chunk, 0)
+    for c in range(later):
+        for part in range(PIECES * c // later, PIECES * (c + 1) // later):
+            product(ready, 0, part)
+        chunk(jnp.int32(ahead + c), 0)
 
     def step(i, carry):
         following = jnp.minimum(i + 1, steps - 1)
@@ -369,7 +374,7 @@
             panel_pos,
             panel_area,
             jnp.pad(observers, ((0, 0), (0, SLOTS - OBSERVERS))),
-            owner.astype(F32).reshape(1, SLOTS),
+            owner.reshape(1, SLOTS).astype(F32),
         ],
         axis=0,
     )

time: 72.2 us -> 71.6 us (level)
  no operation moved by 1% of the time
where the time goes in v5:
time: 71.6 us; the launch traced here: 70.6 us
  Pallas kernels  42.2 us (59%)
  blocking collectives  21.8 us (30%)
  starting transfers between devices  3.72 us (5%)
  other arithmetic  1.53 us (2%)
  local copies, waits for them, and re-layouts  1.31 us (2%)
    pallas_call x1, Pallas kernels, on_device(): pl.pallas_call(field_kernel, out_shape=shape(64, 2, 128), in_specs=[whole...  25.8 us
    all_to_all x1, blocking collectives, on_device(): lax.all_to_all(chunks, ('panel', 'obs'), split_axis=0, concat_axis=0, axi...  21.8 us
    pallas_call x1, Pallas kernels, on_device(): pl.pallas_call(geometry_kernel, out_shape=shape(6, HALF, OBSERVERS), in_s...  13.3 us
    ppermute x1, starting transfers between devices, on_device(): from_below = lax.ppermute(up, 'obs', above)  1.68 us
    pallas_call x1, Pallas kernels, on_device(): pl.pallas_call(early_kernel, out_shape=(shape(6, 128 * EARLY, OBSERVERS),...  1.59 us
  transfers between devices with their start and end apart: 4, of which 0 were waited for; matrix products, arithmetic and copies ran while one was open for 0% of the time, Pallas kernels for 21%

profile of v5, /device:TPU:25, one launch (start us, length us, event | category | flops | bytes accessed | tf_op | source)
XLA Modules:
  0.0 70.6 jit_solution(3964331411916505826)
XLA Ops:
  0.0 0.7 convert_element_type.8
  0.7 0.8 %fusion.pack_ref = f32[10,2048]{1,0:T(8,128)S(1)} fusion(f32[3,1024]{1,0:T(4,128)} %param.8, f32[1,2048]{1,0:T(1,128)S(1)} %bitcast.4, f32[3,2048]{1,0:T(4,128)} %param.7, f32[3,2048]{1,0:T(4,128)} %param.6), kind=kLoop, calls=%fused_computation.3 | loop fusion | flops 143360 | bytes 151552 | tf_op jit(solution)/shard_map/concatenate | solution.py:372
  1.5 0.0 copy-start
  1.5 1.3 %copy-done = f32[32,5,2048]{2,0,1:T(8,128)S(1)} copy-done((f32[32,5,2048]{2,0,1:T(8,128)S(1)}, f32[32,5,2048]{2,0,1:T(8,128)}, u32[]{:S(2)}) %copy-start) | copy-done | bytes 1310744
  2.9 0.2 sources.1
  3.1 0.8 %collective-permute-start = (f32[128,1024]{1,0:T(8,128)S(1)}, f32[128,1024]{1,0:T(8,128)S(1)}, u32[]{:S(2)}, u32[]{:S(2)}) collective-permute-start(f32[128,1024]{1,0:T(8,128)S(1)} %get-tuple-element.16), channel_id=1, source_target_pairs={{0,1},{1,0},{2,3},{3,2},{4,5},{5,4},{6,7},{7,6},{8,9},{9,8},{10,11... | collective-permute-start | bytes 1572872 | tf_op jit(solution)/shard_map/ppermute | solution.py:400
  3.8 1.6 %early.1 = (f32[6,128,1024]{2,1,0:T(8,128)S(1)}, f32[8,128]{1,0:T(8,128)S(1)}) custom-call(f32[10,2048]{1,0:T(8,128)S(1)} %fusion.pack_ref, f32[8,128]{1,0:T(8,128)S(1)} %get-tuple-element.17.mark_ref), custom_call_target="tpu_custom_call" | custom-call | flops 10485760 | bytes 4194304 | tf_op jit(solution)/shard_map/early/pallas_call | solution.py:403
  5.4 0.0 collective-permute-done.recv_ref
  5.4 0.6 bands.1
  6.0 1.7 %collective-permute-start.1 = (f32[16,4096]{1,0:T(8,128)S(1)}, f32[16,4096]{1,0:T(8,128)S(1)}, u32[]{:S(2)}, u32[]{:S(2)}) collective-permute-start(f32[16,4096]{1,0:T(8,128)S(1)} %get-tuple-element.20), channel_id=1, source_target_pairs={{0,2},{1,3},{2,4},{3,5},{4,6},{5,7},{6,0},{7,1},{8,10},{9,11},{10,... | collective-permute-start | bytes 786440 | tf_op jit(solution)/shard_map/ppermute | solution.py:437
  7.7 0.0 collective-permute-start.2
  7.7 1.3 %collective-permute-start.3 = (f32[16,4096]{1,0:T(8,128)S(1)}, f32[16,4096]{1,0:T(8,128)S(1)}, u32[]{:S(2)}, u32[]{:S(2)}) collective-permute-start(f32[16,4096]{1,0:T(8,128)S(1)} %get-tuple-element.22), channel_id=1, source_target_pairs={{0,4},{1,5},{2,6},{3,7},{4,0},{5,1},{6,2},{7,3},{8,12},{9,13},{10,... | collective-permute-start | bytes 786440 | tf_op jit(solution)/shard_map/ppermute | solution.py:436
  9.0 13.3 %geometry.1.geo_ref = f32[6,1024,1024]{2,1,0:T(8,128)S(1)} custom-call(f32[10,2048]{1,0:T(8,128)S(1)} %fusion.pack_ref, f32[8,128]{1,0:T(8,128)S(1)} %get-tuple-element.23.mark_ref, f32[6,128,1024]{2,1,0:T(8,128)S(1)} %get-tuple-element.24.early_ref), custom_call_target="tpu_custom_call" | custom-call | flops 83886080 | bytes 33554432 | tf_op jit(solution)/shard_map/geometry/pallas_call | solution.py:424
  22.3 0.0 collective-permute-done.1.up_ref
  22.3 0.0 collective-permute-done.2.down_ref
  22.3 0.0 collective-permute-done.3.far_ref
  22.3 25.8 %field.1 = f32[64,2,128]{2,1,0:T(2,128)S(1)} custom-call(f32[16,4096]{1,0:T(8,128)S(1)} %get-tuple-element.19.own_ref, f32[16,4096]{1,0:T(8,128)S(1)} %collective-permute-done.1.up_ref, f32[16,4096]{1,0:T(8,128)S(1)} %collective-permute-done.2.down_ref, f32[16,4096]{1,0:T(8,128)S(1)} %collective-permute-done.3.far_ref, f32[10,2048]{1,0:T(8,128)S(1)} %fusion.pack_ref, ...), custom_call_target="tpu_custom_call" | custom-call | tf_op jit(solution)/shard_map/field/pallas_call | solution.py:440
  48.1 21.8 %all_to_all.5.parts_ref = f32[64,2,128]{2,1,0:T(2,128)S(1)} all-to-all(f32[64,2,128]{2,1,0:T(2,128)S(1)} %field.1), channel_id=1, replica_groups={{0,1,8,9,16,17,24,25,32,33,40,41,48,49,56,57,64,65,72,73,80,81,88,89,96..., dimensions={0} | all-to-all | bytes 131072 | tf_op jit(solution)/shard_map/all_to_all | solution.py:460
  69.9 0.7 %finish.1 = f32[2,4,32]{2,1,0:T(4,128)} custom-call(f32[64,2,128]{2,1,0:T(2,128)S(1)} %all_to_all.5.parts_ref), custom_call_target="tpu_custom_call" | custom-call | tf_op jit(solution)/shard_map/finish/pallas_call | solution.py:468
  (1 shorter events, 0.0 us)
Async XLA Ops:
  1.5 1.3 %copy-start = (f32[32,5,2048]{2,0,1:T(8,128)S(1)}, f32[32,5,2048]{2,0,1:T(8,128)}, u32[]{:S(2)}) copy-start(f32[32,5,2048]{2,0,1:T(8,128)} %param.5) | copy-start | bytes 3932164
  3.1 2.4 %collective-permute-start = (f32[128,1024]{1,0:T(8,128)S(1)}, f32[128,1024]{1,0:T(8,128)S(1)}, u32[]{:S(2)}, u32[]{:S(2)}) collective-permute-start(f32[128,1024]{1,0:T(8,128)S(1)} %get-tuple-element.16), channel_id=1, source_target_pairs={{0,1},{1,0},{2,3},{3,2},{4,5},{5,4},{6,7},{7,6},{8,9},{9,8},{10,11... | collective-permute-start | bytes 1572872 | tf_op jit(solution)/shard_map/ppermute | solution.py:400
  6.0 16.3 %collective-permute-start.1 = (f32[16,4096]{1,0:T(8,128)S(1)}, f32[16,4096]{1,0:T(8,128)S(1)}, u32[]{:S(2)}, u32[]{:S(2)}) collective-permute-start(f32[16,4096]{1,0:T(8,128)S(1)} %get-tuple-element.20), channel_id=1, source_target_pairs={{0,2},{1,3},{2,4},{3,5},{4,6},{5,7},{6,0},{7,1},{8,10},{9,11},{10,... | collective-permute-start | bytes 786440 | tf_op jit(solution)/shard_map/ppermute | solution.py:437
  7.7 14.6 %collective-permute-start.2 = (f32[16,4096]{1,0:T(8,128)S(1)}, f32[16,4096]{1,0:T(8,128)S(1)}, u32[]{:S(2)}, u32[]{:S(2)}) collective-permute-start(f32[16,4096]{1,0:T(8,128)S(1)} %get-tuple-element.21), channel_id=1, source_target_pairs={{0,6},{1,7},{2,0},{3,1},{4,2},{5,3},{6,4},{7,5},{8,14},{9,15},{10,... | collective-permute-start | bytes 786440 | tf_op jit(solution)/shard_map/ppermute | solution.py:438
  7.7 14.6 %collective-permute-start.3 = (f32[16,4096]{1,0:T(8,128)S(1)}, f32[16,4096]{1,0:T(8,128)S(1)}, u32[]{:S(2)}, u32[]{:S(2)}) collective-permute-start(f32[16,4096]{1,0:T(8,128)S(1)} %get-tuple-element.22), channel_id=1, source_target_pairs={{0,4},{1,5},{2,6},{3,7},{4,0},{5,1},{6,2},{7,3},{8,12},{9,13},{10,... | collective-permute-start | bytes 786440 | tf_op jit(solution)/shard_map/ppermute | solution.py:436

commit v6 on v5

--- a/solution.py
+++ b/solution.py
@@ -181,8 +181,9 @@
                 if power == 2:
                     cr, ci = double(cr, ci)
                 elif power == 3:
-                    dr, di = double(cr, ci)
-                    cr, ci = cr * dr - ci * di, cr * di + ci * dr
+                    twice = cr + cr
+                    fourth = twice * twice
+                    cr, ci = cr * (fourth - 3.0), ci * (fourth - 1.0)
                 gr, gi = amp * cr, amp * ci
             br, bi = (gr * er, gr * ei) if power == 0 else (gr * er - gi * ei, gr * ei + gi * er)
             for i, value in enumerate((r, er + er, gr, gi, br, bi)):

time: 71.6 us -> 71.5 us (level)
  the two profiles are of different devices: /device:TPU:25 before, /device:TPU:1 now
where the time goes in v6:
time: 71.5 us; the launch traced here: 71.3 us
  Pallas kernels  37.8 us (53%)
  blocking collectives  22.2 us (31%)
  starting transfers between devices  6.08 us (9%)
  waiting for transfers between devices  2.27 us (3%)
  other arithmetic  1.53 us (2%)
  local copies, waits for them, and re-layouts  1.31 us (2%)
    pallas_call x1, Pallas kernels, on_device(): pl.pallas_call(field_kernel, out_shape=shape(64, 2, 128), in_specs=[whole...  25.8 us
    all_to_all x1, blocking collectives, on_device(): lax.all_to_all(chunks, ('panel', 'obs'), split_axis=0, concat_axis=0, axi...  22.2 us
    pallas_call x1, Pallas kernels, on_device(): pl.pallas_call(geometry_kernel, out_shape=shape(6, HALF, OBSERVERS), in_s...  9.28 us
    ppermute x1, starting transfers between devices, on_device(): recv = lax.ppermute(send, 'obs', swap)  3.33 us
    ppermute x1, starting transfers between devices, on_device(): from_above = lax.ppermute(down, 'obs', below)  2.66 us
    ppermute x1, waiting for transfers between devices, on_device(): across = lax.ppermute(far, 'obs', [(i, (i + 4) % 8) for i in range(8)])  1.86 us
  transfers between devices with their start and end apart: 4, of which 2 were waited for; matrix products, arithmetic and copies ran while one was open for 0% of the time, Pallas kernels for 15%

profile of v6, /device:TPU:1, one launch (start us, length us, event | category | flops | bytes accessed | tf_op | source)
XLA Modules:
  0.0 71.3 jit_solution(3404888474788462919)
XLA Ops:
  0.0 0.7 convert_element_type.8
  0.7 0.8 %fusion.pack_ref = f32[10,2048]{1,0:T(8,128)S(1)} fusion(f32[3,1024]{1,0:T(4,128)} %param.8, f32[1,2048]{1,0:T(1,128)S(1)} %bitcast.4, f32[3,2048]{1,0:T(4,128)} %param.7, f32[3,2048]{1,0:T(4,128)} %param.6), kind=kLoop, calls=%fused_computation.3 | loop fusion | flops 143360 | bytes 151552 | tf_op jit(solution)/shard_map/concatenate | solution.py:373
  1.5 0.0 copy-start
  1.5 1.3 %copy-done = f32[32,5,2048]{2,0,1:T(8,128)S(1)} copy-done((f32[32,5,2048]{2,0,1:T(8,128)S(1)}, f32[32,5,2048]{2,0,1:T(8,128)}, u32[]{:S(2)}) %copy-start) | copy-done | bytes 1310744
  2.9 0.2 sources.1
  3.1 3.3 %collective-permute-start = (f32[128,1024]{1,0:T(8,128)S(1)}, f32[128,1024]{1,0:T(8,128)S(1)}, u32[]{:S(2)}, u32[]{:S(2)}) collective-permute-start(f32[128,1024]{1,0:T(8,128)S(1)} %get-tuple-element.16), channel_id=1, source_target_pairs={{0,1},{1,0},{2,3},{3,2},{4,5},{5,4},{6,7},{7,6},{8,9},{9,8},{10,11... | collective-permute-start | bytes 1572872 | tf_op jit(solution)/shard_map/ppermute | solution.py:401
  6.4 1.1 %early.1 = (f32[6,128,1024]{2,1,0:T(8,128)S(1)}, f32[8,128]{1,0:T(8,128)S(1)}) custom-call(f32[10,2048]{1,0:T(8,128)S(1)} %fusion.pack_ref, f32[8,128]{1,0:T(8,128)S(1)} %get-tuple-element.17.mark_ref), custom_call_target="tpu_custom_call" | custom-call | flops 10485760 | bytes 4194304 | tf_op jit(solution)/shard_map/early/pallas_call | solution.py:404
  7.5 0.4 collective-permute-done.recv_ref
  7.9 0.6 bands.1
  8.5 0.1 collective-permute-start.1
  8.6 2.7 %collective-permute-start.2 = (f32[16,4096]{1,0:T(8,128)S(1)}, f32[16,4096]{1,0:T(8,128)S(1)}, u32[]{:S(2)}, u32[]{:S(2)}) collective-permute-start(f32[16,4096]{1,0:T(8,128)S(1)} %get-tuple-element.21), channel_id=1, source_target_pairs={{0,6},{1,7},{2,0},{3,1},{4,2},{5,3},{6,4},{7,5},{8,14},{9,15},{10,... | collective-permute-start | bytes 786440 | tf_op jit(solution)/shard_map/ppermute | solution.py:439
  11.2 0.0 collective-permute-start.3
  11.3 9.3 %geometry.1.geo_ref = f32[6,1024,1024]{2,1,0:T(8,128)S(1)} custom-call(f32[10,2048]{1,0:T(8,128)S(1)} %fusion.pack_ref, f32[8,128]{1,0:T(8,128)S(1)} %get-tuple-element.23.mark_ref, f32[6,128,1024]{2,1,0:T(8,128)S(1)} %get-tuple-element.24.early_ref), custom_call_target="tpu_custom_call" | custom-call | flops 83886080 | bytes 33554432 | tf_op jit(solution)/shard_map/geometry/pallas_call | solution.py:425
  20.6 0.0 collective-permute-done.1.up_ref
  20.6 0.0 collective-permute-done.2.down_ref
  20.6 1.9 %collective-permute-done.3.far_ref = f32[16,4096]{1,0:T(8,128)S(1)} collective-permute-done((f32[16,4096]{1,0:T(8,128)S(1)}, f32[16,4096]{1,0:T(8,128)S(1)}, u32[]{:S(2)}, u32[]{:S(2)}) %collective-permute-start.3) | collective-permute-done | bytes 262176 | tf_op jit(solution)/shard_map/ppermute | solution.py:437
  22.5 25.8 %field.1 = f32[64,2,128]{2,1,0:T(2,128)S(1)} custom-call(f32[16,4096]{1,0:T(8,128)S(1)} %get-tuple-element.19.own_ref, f32[16,4096]{1,0:T(8,128)S(1)} %collective-permute-done.1.up_ref, f32[16,4096]{1,0:T(8,128)S(1)} %collective-permute-done.2.down_ref, f32[16,4096]{1,0:T(8,128)S(1)} %collective-permute-done.3.far_ref, f32[10,2048]{1,0:T(8,128)S(1)} %fusion.pack_ref, ...), custom_call_target="tpu_custom_call" | custom-call | tf_op jit(solution)/shard_map/field/pallas_call | solution.py:441
  48.3 22.2 %all_to_all.5.parts_ref = f32[64,2,128]{2,1,0:T(2,128)S(1)} all-to-all(f32[64,2,128]{2,1,0:T(2,128)S(1)} %field.1), channel_id=1, replica_groups={{0,1,8,9,16,17,24,25,32,33,40,41,48,49,56,57,64,65,72,73,80,81,88,89,96..., dimensions={0} | all-to-all | bytes 131072 | tf_op jit(solution)/shard_map/all_to_all | solution.py:461
  70.5 0.7 %finish.1 = f32[2,4,32]{2,1,0:T(4,128)} custom-call(f32[64,2,128]{2,1,0:T(2,128)S(1)} %all_to_all.5.parts_ref), custom_call_target="tpu_custom_call" | custom-call | tf_op jit(solution)/shard_map/finish/pallas_call | solution.py:469
  (1 shorter events, 0.0 us)
Async XLA Ops:
  1.5 1.3 %copy-start = (f32[32,5,2048]{2,0,1:T(8,128)S(1)}, f32[32,5,2048]{2,0,1:T(8,128)}, u32[]{:S(2)}) copy-start(f32[32,5,2048]{2,0,1:T(8,128)} %param.5) | copy-start | bytes 3932164
  3.1 4.9 %collective-permute-start = (f32[128,1024]{1,0:T(8,128)S(1)}, f32[128,1024]{1,0:T(8,128)S(1)}, u32[]{:S(2)}, u32[]{:S(2)}) collective-permute-start(f32[128,1024]{1,0:T(8,128)S(1)} %get-tuple-element.16), channel_id=1, source_target_pairs={{0,1},{1,0},{2,3},{3,2},{4,5},{5,4},{6,7},{7,6},{8,9},{9,8},{10,11... | collective-permute-start | bytes 1572872 | tf_op jit(solution)/shard_map/ppermute | solution.py:401
  8.5 12.1 %collective-permute-start.1 = (f32[16,4096]{1,0:T(8,128)S(1)}, f32[16,4096]{1,0:T(8,128)S(1)}, u32[]{:S(2)}, u32[]{:S(2)}) collective-permute-start(f32[16,4096]{1,0:T(8,128)S(1)} %get-tuple-element.20), channel_id=1, source_target_pairs={{0,2},{1,3},{2,4},{3,5},{4,6},{5,7},{6,0},{7,1},{8,10},{9,11},{10,... | collective-permute-start | bytes 786440 | tf_op jit(solution)/shard_map/ppermute | solution.py:438
  8.6 12.0 %collective-permute-start.2 = (f32[16,4096]{1,0:T(8,128)S(1)}, f32[16,4096]{1,0:T(8,128)S(1)}, u32[]{:S(2)}, u32[]{:S(2)}) collective-permute-start(f32[16,4096]{1,0:T(8,128)S(1)} %get-tuple-element.21), channel_id=1, source_target_pairs={{0,6},{1,7},{2,0},{3,1},{4,2},{5,3},{6,4},{7,5},{8,14},{9,15},{10,... | collective-permute-start | bytes 786440 | tf_op jit(solution)/shard_map/ppermute | solution.py:439
  11.2 11.2 %collective-permute-start.3 = (f32[16,4096]{1,0:T(8,128)S(1)}, f32[16,4096]{1,0:T(8,128)S(1)}, u32[]{:S(2)}, u32[]{:S(2)}) collective-permute-start(f32[16,4096]{1,0:T(8,128)S(1)} %get-tuple-element.22), channel_id=1, source_target_pairs={{0,4},{1,5},{2,6},{3,7},{4,0},{5,1},{6,2},{7,3},{8,12},{9,13},{10,... | collective-permute-start | bytes 786440 | tf_op jit(solution)/shard_map/ppermute | solution.py:437
